TPU v7x, 256 devices: a whole 4x4x8 slice. The times are simulated.
256 devices in a mesh: blk: 32 (over z, x_hi, core), rep: 8 (over x_lo, y).
Axes of the slice: x: 4 (x_hi: 2, x_lo: 2; x = x_hi * 2 + x_lo), y: 4, z: 8, core: 2. Of those that a mesh axis runs over, the one named last changes fastest.
Arguments:
- node_features: bfloat16 [65536, 256], P(('blk', 'rep')), may hold values from -6 to 6
- weight: bfloat16 [256, 256], replicated, may hold values from -0.375 to 0.375
- cotangent: bfloat16 [65536, 256], P(('blk', 'rep')), may hold values from -6 to 6
- tile_values: int32 [32, 8, 32, 4, 128, 128], P('blk', 'rep'), may hold values from 0 to 5
- tile_rows: int32 [32, 8, 32, 4], P('blk', 'rep'), may hold values from 0 to 15, as said below
- tile_cols: int32 [32, 8, 32, 4], P('blk', 'rep'), may hold values from 0 to 1, as said below
- tile_count: int32 [32, 8, 32], P('blk', 'rep'), may hold values from 0 to 4, as said below
Outputs:
- activations: bfloat16 [65536, 256], P(('blk', 'rep'))
- feature_grad: bfloat16 [65536, 256], P(('blk', 'rep'))
- weight_grad: float32 [256, 256], replicated
Inputs may be any that keep to these rules, and one draw needn't show every extreme that they name: Within one row group, column share and column group, the pairs (tile_rows, tile_cols) of the 4 slots are distinct. `tile_cols`: see tile_rows. `tile_count`: some entry equals 4 in every draw.
All inputs are finite; a program needn't handle non-finite values.
Results may differ from a plain program's by a relative error of at most 0.0064.
Values may be sent and summed in bfloat16 or wider, within the bound.
A program may use at most 64 MiB of HBM per device.

v0:
```python
import jax
import jax.numpy as jnp
from jax import lax
from jax.sharding import PartitionSpec as P


def shifted(array, axis, by):
    count = lax.axis_size(axis)
    return lax.ppermute(array, axis, [(i, (i + by) % count) for i in range(count)])


def shards(node_features, weight, cotangent, tile_values, tile_rows, tile_cols, tile_count):
    groups = lax.axis_size("blk")
    replicas = lax.axis_size("rep")
    cycle_index = lax.axis_index("blk")
    node_dev, feature_width = node_features.shape
    tile_size = tile_values.shape[-1]
    slot_count = tile_values.shape[3]
    row_tiles = node_dev * replicas // tile_size
    col_tiles = node_dev // tile_size
    n_nodes = node_dev * groups * replicas
    live_mask = jnp.arange(slot_count, dtype=jnp.int32) < tile_count[0, 0][:, None]
    blocks = jnp.where(live_mask[..., None, None], tile_values[0, 0], 0).astype(jnp.bfloat16)
    row_ids = tile_rows[0, 0]
    col_ids = tile_cols[0, 0]
    row_totals = jnp.sum(blocks, axis=-1, dtype=jnp.float32)
    degree_part = jnp.zeros((row_tiles, tile_size), jnp.float32)
    degree_part = (
        degree_part.at[row_ids.reshape(-1)].add(row_totals.reshape(-1, tile_size)).reshape(-1)
    )

    def add_group(partial_rows, features, group):
        group_blocks = lax.dynamic_index_in_dim(blocks, group, 0, keepdims=False)
        group_rows = lax.dynamic_index_in_dim(row_ids, group, 0, keepdims=False)
        group_cols = lax.dynamic_index_in_dim(col_ids, group, 0, keepdims=False)
        picked = features.reshape(col_tiles, tile_size, feature_width)[group_cols]
        product = jnp.einsum(
            "sab,sbf->saf", group_blocks, picked, preferred_element_type=jnp.float32
        )
        return partial_rows.at[group_rows].add(product)

    empty_rows = jnp.zeros((row_tiles, tile_size, feature_width), jnp.float32)

    def forward_step(step_num, carried):
        features, partial_rows = carried
        partial_rows = add_group(partial_rows, features, (cycle_index - step_num) % groups)
        features = shifted(features, "blk", 1)
        return (features, partial_rows)

    features, partial_rows = lax.fori_loop(0, groups - 1, forward_step, (node_features, empty_rows))
    partial_rows = add_group(partial_rows, features, (cycle_index - groups + 1) % groups)
    summed, degree = (
        lax.psum_scatter(
            partial_rows.reshape(-1, feature_width), "rep", scatter_dimension=0, tiled=True
        ),
        lax.psum_scatter(degree_part, "rep", scatter_dimension=0, tiled=True),
    )
    norm_scale = lax.rsqrt(degree + 1.0)[:, None]
    mixed = ((summed + node_features.astype(jnp.float32)) * norm_scale).astype(jnp.bfloat16)
    pre_act = jnp.dot(mixed, weight, preferred_element_type=jnp.float32)
    activations = jax.nn.silu(pre_act).astype(jnp.bfloat16)
    sigmoid_pre = jax.nn.sigmoid(pre_act)
    act_grad = (
        cotangent.astype(jnp.float32) * sigmoid_pre * (1.0 + pre_act * (1.0 - sigmoid_pre))
    ).astype(jnp.bfloat16)
    weight_part = jnp.einsum("nf,ng->fg", mixed, act_grad, preferred_element_type=jnp.float32)
    weight_grad = lax.psum(weight_part, ("blk", "rep")) * n_nodes ** (-0.5)
    back_proj = jnp.einsum("ng,fg->nf", act_grad, weight, preferred_element_type=jnp.float32)
    node_grad = (back_proj * norm_scale).astype(jnp.bfloat16)
    group_grad = lax.all_gather(node_grad, "rep", axis=0, tiled=True).reshape(
        row_tiles, tile_size, feature_width
    )

    def group_term(target):
        target_blocks = lax.dynamic_index_in_dim(blocks, target, 0, keepdims=False)
        target_rows = lax.dynamic_index_in_dim(row_ids, target, 0, keepdims=False)
        target_cols = lax.dynamic_index_in_dim(col_ids, target, 0, keepdims=False)
        picked = group_grad[target_rows]
        product = jnp.einsum(
            "sab,saf->sbf", target_blocks, picked, preferred_element_type=jnp.float32
        )
        placed = (
            jnp.zeros((col_tiles, tile_size, feature_width), jnp.float32)
            .at[target_cols]
            .add(product)
        )
        return placed.reshape(node_dev, feature_width)

    def backward_step(step_num, carried_sum):
        carried_sum = carried_sum + group_term((cycle_index - step_num - 1) % groups)
        return shifted(carried_sum, "blk", 1)

    carried_sum = lax.fori_loop(
        0, groups - 1, backward_step, jnp.zeros((node_dev, feature_width), jnp.float32)
    )
    gathered_sum = carried_sum + group_term(cycle_index)
    feature_grad = (gathered_sum + node_grad.astype(jnp.float32)).astype(jnp.bfloat16)
    return (activations, feature_grad, weight_grad)


def solution(mesh):
    in_specs = (
        P(("blk", "rep"), None),
        P(),
        P(("blk", "rep"), None),
        P("blk", "rep", None, None, None, None),
        P("blk", "rep", None, None),
        P("blk", "rep", None, None),
        P("blk", "rep", None),
    )
    out_specs = (P(("blk", "rep"), None), P(("blk", "rep"), None), P())
    return jax.shard_map(shards, mesh=mesh, in_specs=in_specs, out_specs=out_specs, check_vma=False)
```

profile of v0, /device:TPU:8, one launch (start us, length us, event | category | flops | bytes accessed | tf_op | source)
XLA Modules:
  0.0 1047.2 jit_solution(5072869990157165632)
XLA Ops:
  9.3 9.0 copy.26
  18.5 5.5 convert_reduce_fusion
  24.2 253.5 %while.32 = (s32[]{:T(128)}, bf16[256,256]{1,0:T(8,128)(2,1)S(1)}, f32[16,128,256]{2,1,0:T(8,128)S(1)}, s32[]{:T(128)}, s32[32,4]{1,0:T(8,128)S(1)}, /*index=5*/...) while((s32[]{:T(128)}, bf16[256,256]{1,0:T(8,128)(2,1)S(1)}, ...), condition=%wide.region_2.3_spmd, body=%wide.region_0.0_spmd.sunk | while | flops 33686568 | bytes 3805608 | solution.py:50
  27.0 7.7 collective-permute-done
  69.9 5.3 collective-permute-done
  86.1 5.3 collective-permute-done
  134.7 5.3 collective-permute-done
  150.9 5.3 collective-permute-done
  175.2 5.3 collective-permute-done
  183.3 5.3 collective-permute-done
  215.7 5.3 collective-permute-done
  240.0 5.3 collective-permute-done
  284.2 16.9 %all-reduce = f32[2048]{0:T(1024)S(1)} all-reduce(f32[2048]{0:T(1024)S(1)} %bitcast.126), channel_id=3, replica_groups=mesh['blk'=32,'rep'=8] {'rep'}, use_global_device_ids=true, to_apply=%region_7.8.clone | all-reduce | flops 2048 | bytes 16384
  301.2 21.6 %reduce-scatter.2.cloned.1.call-done = f32[256,256]{1,0:T(8,128)} async-done(((f32[2048,256]{1,0:T(8,128)}), f32[256,256]{1,0:T(8,128)}) %reduce-scatter.2.cloned.1.call-update) | async-done | bytes 262160 | tf_op jit(solution)/shard_map/reduce_scatter | solution.py:53
  326.7 254.3 %all-reduce.3.cloned.1.call-done = f32[256,256]{1,0:T(8,128)} async-done(((f32[256,256]{1,0:T(8,128)}), f32[256,256]{1,0:T(8,128)}) %all-reduce.3.cloned.1.call-update) | async-done | bytes 262160 | tf_op jit(solution)/shard_map/psum | solution.py:67
  582.7 38.6 %all-gather.2.cloned.1.call-done = bf16[2048,256]{1,0:T(8,128)(2,1)} async-done(((bf16[256,256]{1,0:T(8,128)(2,1)}), bf16[2048,256]{1,0:T(8,128)(2,1)}) %all-gather.2.cloned.1.call-update) | async-done | bytes 1048592 | tf_op jit(solution)/shard_map/all_gather | solution.py:70
  625.2 414.8 %while.33 = (s32[]{:T(128)}, f32[256,256]{1,0:T(8,128)S(1)}, s32[]{:T(128)}, s32[32,4]{1,0:T(8,128)S(1)}, bf16[32,4,128,128]{2,3,1,0:T(8,128)(2,1)}, /*index=5*/...) while((s32[]{:T(128)}, f32[256,256]{1,0:T(8,128)S(1)}, ...), condition=%wide.region_10.11_spmd, body=%wide.region_8.10_spmd.sunk | while | flops 33752104 | bytes 5116360 | solution.py:93
  629.2 9.4 collective-permute-done.1
  642.6 9.4 collective-permute-done.1
  656.0 9.4 collective-permute-done.1
  669.3 9.4 collective-permute-done.1
  682.7 9.4 collective-permute-done.1
  696.1 9.4 collective-permute-done.1
  709.5 9.4 collective-permute-done.1
  722.8 9.4 collective-permute-done.1
  736.2 9.4 collective-permute-done.1
  749.6 9.4 collective-permute-done.1
  763.0 9.4 collective-permute-done.1
  776.3 9.4 collective-permute-done.1
  789.7 9.4 collective-permute-done.1
  803.1 9.4 collective-permute-done.1
  816.5 9.4 collective-permute-done.1
  829.9 9.4 collective-permute-done.1
  843.2 9.4 collective-permute-done.1
  856.6 9.4 collective-permute-done.1
  870.0 9.4 collective-permute-done.1
  883.4 9.4 collective-permute-done.1
  896.8 9.4 collective-permute-done.1
  910.1 9.4 collective-permute-done.1
  923.5 9.4 collective-permute-done.1
  936.9 9.4 collective-permute-done.1
  950.3 9.4 collective-permute-done.1
  963.7 9.4 collective-permute-done.1
  977.0 9.4 collective-permute-done.1
  990.4 9.4 collective-permute-done.1
  1003.8 9.4 collective-permute-done.1
  1017.2 9.4 collective-permute-done.1
  1030.6 9.4 collective-permute-done.1
  (544 shorter events, 341.2 us)
Async XLA Ops:
  7.2 315.6 %reduce-scatter.2.cloned.1.call-start = ((), (), s32[]{:S(2)}) async-start(), calls=%async_computation.1 | async-start | bytes 2359296 | tf_op jit(solution)/shard_map/reduce_scatter | solution.py:53
  24.2 10.5 %collective-permute-start = (bf16[256,256]{1,0:T(8,128)(2,1)S(1)}, bf16[256,256]{1,0:T(8,128)(2,1)S(1)}, u32[]{:S(2)}, u32[]{:S(2)}) collective-permute-start(bf16[256,256]{1,0:T(8,128)(2,1)S(1)} %copy.41), channel_id=1, source_target_pairs={{0,8},{8,16},{16,24},{24,32},{32,40},{40,48},{48,56},{56,64},{64,7... | collective-permute-start | bytes 393224 | tf_op jit(solution)/shard_map/while/body/eval_jaxpr/ppermute | solution.py:9
  34.7 8.1 collective-permute-start
  59.0 8.1 collective-permute-start
  67.1 8.1 collective-permute-start
  91.4 8.1 collective-permute-start
  99.5 8.1 collective-permute-start
  123.8 8.1 collective-permute-start
  131.9 8.1 collective-permute-start
  148.1 8.1 collective-permute-start
  156.2 8.1 collective-permute-start
  180.5 8.1 collective-permute-start
  188.6 8.1 collective-permute-start
  212.9 8.1 collective-permute-start
  221.0 8.1 collective-permute-start
  281.7 299.3 %all-reduce.3.cloned.1.call-start = ((), (), s32[]{:S(2)}) async-start(), calls=%async_computation.3 | async-start | bytes 524288 | tf_op jit(solution)/shard_map/psum | solution.py:67
  325.7 295.6 %all-gather.2.cloned.1.call-start = ((), (), s32[]{:S(2)}) async-start(), calls=%async_computation.2 | async-start | bytes 1179648 | tf_op jit(solution)/shard_map/all_gather | solution.py:70
  629.1 9.5 collective-permute-start.1
  642.5 9.5 collective-permute-start.1
  655.9 9.5 collective-permute-start.1
  669.2 9.5 collective-permute-start.1
  682.6 9.5 collective-permute-start.1
  696.0 9.5 collective-permute-start.1
  709.4 9.5 collective-permute-start.1
  722.8 9.5 collective-permute-start.1
  736.1 9.5 collective-permute-start.1
  749.5 9.5 collective-permute-start.1
  762.9 9.5 collective-permute-start.1
  776.3 9.5 collective-permute-start.1
  789.6 9.5 collective-permute-start.1
  803.0 9.5 collective-permute-start.1
  816.4 9.5 collective-permute-start.1
  829.8 9.5 collective-permute-start.1
  843.1 9.5 collective-permute-start.1
  856.5 9.5 collective-permute-start.1
  869.9 9.5 collective-permute-start.1
  883.3 9.5 collective-permute-start.1
  896.7 9.5 collective-permute-start.1
  910.0 9.5 collective-permute-start.1
  923.4 9.5 collective-permute-start.1
  936.8 9.5 collective-permute-start.1
  950.2 9.5 collective-permute-start.1
  963.6 9.5 collective-permute-start.1
  976.9 9.5 collective-permute-start.1
  990.3 9.5 collective-permute-start.1
  1003.7 9.5 collective-permute-start.1
  1017.1 9.5 collective-permute-start.1
  1030.5 9.5 collective-permute-start.1
  (27 other events, 998.7 us)
Sparse Core Ops, SparseCore 0:
  281.8 40.8 reduce-scatter.1
  328.8 252.1 all-reduce.2
  583.4 37.8 all-gather.1
where the time goes:
time: 1050 us
  waiting for transfers between devices  772 us (74%)
  local copies, waits for them, and re-layouts  89.6 us (9%)
  matrix products  75.9 us (7%)
  other arithmetic  68.5 us (7%)
  blocking collectives  16.9 us (2%)
  between operations  14.7 us (1%)
    ppermute x62, waiting for transfers between devices, shifted(): lax.ppermute(array, axis, [(i, (i + by) % count) for i in range(count)])  457 us
    psum x1, waiting for transfers between devices, shards(): weight_grad = lax.psum(weight_part, ('blk', 'rep')) * n_nodes ** (-0.5)  254 us
    gather x32, local copies, waits for them, and re-layouts, group_term(): picked = group_grad[target_rows]  57.2 us
    all_gather x1, waiting for transfers between devices, shards(): lax.all_gather(node_grad, 'rep', axis=0, tiled=True)  38.6 us
    dot_general x32, matrix products, add_group(): jnp.einsum('sab,sbf->saf', group_blocks, picked, preferred_element_type=j...  37.5 us
    dot_general x32, matrix products, group_term(): jnp.einsum('sab,saf->sbf', target_blocks, picked, preferred_element_type=...  35.6 us
    scatter-add x32, other arithmetic, add_group(): return partial_rows.at[group_rows].add(product)  28.4 us
    scatter-add x32, other arithmetic, group_term(): placed = jnp.zeros((col_tiles, tile_size, feature_width), jnp.float32).at...  27.9 us
  transfers between devices with their start and end apart: 65, of which 65 were waited for; matrix products, arithmetic and copies ran while one was open for 8% of the time, Pallas kernels for 0%

commit v1 on v0

v1 whole, which is shorter than its diff:
```python
import jax
import jax.numpy as jnp
from jax import lax
from jax.experimental import pallas as pl
from jax.experimental.pallas import tpu as pltpu
from jax.sharding import PartitionSpec as P

TILE = 128
SLOT = 4


def forward_kernel(rows_ref, cols_ref, count_ref, tiles_ref, feat_ref, sum_ref, deg_ref, kept_ref):
    j = pl.program_id(0)

    @pl.when(j == 0)
    def _():
        sum_ref[...] = jnp.zeros_like(sum_ref)
        deg_ref[...] = jnp.zeros_like(deg_ref)

    for s in range(SLOT):
        live = s < count_ref[j]
        tile = jnp.where(live, tiles_ref[0, s], 0).astype(jnp.float32)
        row = rows_ref[j * SLOT + s]
        col = cols_ref[j * SLOT + s]
        kept = tile.astype(jnp.bfloat16)
        kept_ref[0, s] = kept
        feat = feat_ref[0, pl.ds(pl.multiple_of(col * TILE, TILE), TILE), :]
        sum_ref[row] += jnp.dot(kept, feat, preferred_element_type=jnp.float32)
        deg_ref[row] += jnp.sum(tile, axis=1, keepdims=True)


def backward_kernel(rows_ref, cols_ref, tiles_ref, grad_ref, out_ref):
    j = pl.program_id(0)
    out_ref[...] = jnp.zeros_like(out_ref)
    for s in range(SLOT):
        row = rows_ref[j * SLOT + s]
        col = cols_ref[j * SLOT + s]
        term = lax.dot_general(
            tiles_ref[0, s], grad_ref[row], (((0,), (0,)), ((), ())),
            preferred_element_type=jnp.float32)
        out_ref[0, col] += term


def shards(node_features, weight, cotangent, tile_values, tile_rows, tile_cols, tile_count):
    groups = lax.axis_size("blk")
    replicas = lax.axis_size("rep")
    node_dev, width = node_features.shape
    row_tiles = node_dev * replicas // TILE
    col_tiles = node_dev // TILE
    n_nodes = node_dev * groups * replicas
    rows = tile_rows.reshape(-1)
    cols = tile_cols.reshape(-1)
    count = tile_count.reshape(-1)
    feats = lax.all_gather(node_features, "blk", axis=0, tiled=False)
    summed, degree, kept = pl.pallas_call(
        forward_kernel,
        grid_spec=pltpu.PrefetchScalarGridSpec(
            num_scalar_prefetch=3,
            grid=(groups,),
            in_specs=[
                pl.BlockSpec((1, SLOT, TILE, TILE), lambda j, *_: (j, 0, 0, 0)),
                pl.BlockSpec((1, node_dev, width), lambda j, *_: (j, 0, 0)),
            ],
            out_specs=[
                pl.BlockSpec((row_tiles, TILE, width), lambda j, *_: (0, 0, 0)),
                pl.BlockSpec((row_tiles, TILE, 1), lambda j, *_: (0, 0, 0)),
                pl.BlockSpec((1, SLOT, TILE, TILE), lambda j, *_: (j, 0, 0, 0)),
            ],
        ),
        out_shape=[
            jax.ShapeDtypeStruct((row_tiles, TILE, width), jnp.float32),
            jax.ShapeDtypeStruct((row_tiles, TILE, 1), jnp.float32),
            jax.ShapeDtypeStruct((groups, SLOT, TILE, TILE), jnp.bfloat16),
        ],
        compiler_params=pltpu.CompilerParams(vmem_limit_bytes=32 << 20),
    )(rows, cols, count, tile_values[0, 0], feats)
    summed = lax.psum_scatter(summed.reshape(-1, width), "rep", scatter_dimension=0, tiled=True)
    degree = lax.psum_scatter(degree.reshape(-1), "rep", scatter_dimension=0, tiled=True)
    scale = lax.rsqrt(degree + 1.0)[:, None]
    mixed = ((summed + node_features.astype(jnp.float32)) * scale).astype(jnp.bfloat16)
    pre = jnp.dot(mixed, weight, preferred_element_type=jnp.float32)
    sig = jax.nn.sigmoid(pre)
    activations = (pre * sig).astype(jnp.bfloat16)
    act_grad = (cotangent.astype(jnp.float32) * sig * (1.0 + pre * (1.0 - sig))).astype(jnp.bfloat16)
    weight_part = jnp.einsum("nf,ng->fg", mixed, act_grad, preferred_element_type=jnp.float32)
    weight_grad = lax.psum(weight_part, ("blk", "rep")) * n_nodes ** (-0.5)
    back = jnp.einsum("ng,fg->nf", act_grad, weight, preferred_element_type=jnp.float32)
    node_grad = (back * scale).astype(jnp.bfloat16)
    group_grad = lax.all_gather(node_grad, "rep", axis=0, tiled=True).reshape(row_tiles, TILE, width)
    terms = pl.pallas_call(
        backward_kernel,
        grid_spec=pltpu.PrefetchScalarGridSpec(
            num_scalar_prefetch=2,
            grid=(groups,),
            in_specs=[
                pl.BlockSpec((1, SLOT, TILE, TILE), lambda j, *_: (j, 0, 0, 0)),
                pl.BlockSpec((row_tiles, TILE, width), lambda j, *_: (0, 0, 0)),
            ],
            out_specs=pl.BlockSpec((1, col_tiles, TILE, width), lambda j, *_: (j, 0, 0, 0)),
        ),
        out_shape=jax.ShapeDtypeStruct((groups, col_tiles, TILE, width), jnp.float32),
        compiler_params=pltpu.CompilerParams(vmem_limit_bytes=32 << 20),
    )(rows, cols, kept, group_grad)
    spread = lax.psum_scatter(terms.reshape(-1, width), "blk", scatter_dimension=0, tiled=True)
    feature_grad = (spread + node_grad.astype(jnp.float32)).astype(jnp.bfloat16)
    return activations, feature_grad, weight_grad


def solution(mesh):
    in_specs = (
        P(("blk", "rep"), None),
        P(),
        P(("blk", "rep"), None),
        P("blk", "rep", None, None, None, None),
        P("blk", "rep", None, None),
        P("blk", "rep", None, None),
        P("blk", "rep", None),
    )
    out_specs = (P(("blk", "rep"), None), P(("blk", "rep"), None), P())
    return jax.shard_map(shards, mesh=mesh, in_specs=in_specs, out_specs=out_specs, check_vma=False)
```

time: 1050 us -> 625 us (0.60)
  waiting for transfers between devices: 772 us -> 549 us
  matrix products: 75.9 us -> 2.75 us
  local copies, waits for them, and re-layouts: 89.6 us -> 17.1 us
  other arithmetic: 68.5 us -> 4.78 us
  Pallas kernels: 0 us -> 19.5 us
    ppermute x62 -> x0, waiting for transfers between devices: 457 us -> none  [shifted(): lax.ppermute(array, axis, [(i, (i + by) % count) for i in range(count)])]
    reduce_scatter x1 -> x2, waiting for transfers between devices: 21.6 us -> 176 us  [the longest x1 156 us: shards(): lax.psum_scatter(terms.reshape(-1, width), 'blk', scatter_dimension=0, ti...]
    all_gather x0 -> x1, waiting for transfers between devices: none -> 90.8 us  [shards(): feats = lax.all_gather(node_features, 'blk', axis=0, tiled=False)]
    gather x64 -> x0, local copies, waits for them, and re-layouts: 75.2 us -> none  [the longest x32 57.2 us: group_term(): picked = group_grad[target_rows]]
    dot_general x65 -> x1, matrix products: 74.1 us -> 0.94 us  [shards(): pre = jnp.dot(mixed, weight, preferred_element_type=jnp.float32)]
    scatter-add x65 -> x0, other arithmetic: 57.3 us -> none  [the longest x32 28.4 us: add_group(): return partial_rows.at[group_rows].add(product)]
    pallas_call x0 -> x2, Pallas kernels: none -> 19.5 us  [the longest x1 10.2 us: shards(): pl.pallas_call(forward_kernel, grid_spec=pltpu.PrefetchScalarGridSpec(num...]
    psum x1, waiting for transfers between devices: 254 us -> 242 us  [shards(): weight_grad = lax.psum(weight_part, ('blk', 'rep')) * n_nodes ** (-0.5)]
  transfers between devices with their start and end apart: 65 -> 5, of which waited for: 65 -> 5; matrix products, arithmetic and copies ran while one was open for 8% -> 1% of each run, Pallas kernels for 0% -> 1%
where the time goes in v1:
time: 625 us
  waiting for transfers between devices  549 us (88%)
  Pallas kernels  19.5 us (3%)
  local copies, waits for them, and re-layouts  17.1 us (3%)
  blocking collectives  16.9 us (3%)
  between operations  14.5 us (2%)
    psum x1, waiting for transfers between devices, shards(): weight_grad = lax.psum(weight_part, ('blk', 'rep')) * n_nodes ** (-0.5)  242 us
    reduce_scatter x1, waiting for transfers between devices, shards(): lax.psum_scatter(terms.reshape(-1, width), 'blk', scatter_dimension=0, ti...  156 us
    all_gather x1, waiting for transfers between devices, shards(): feats = lax.all_gather(node_features, 'blk', axis=0, tiled=False)  90.8 us
    all_gather x1, waiting for transfers between devices, shards(): lax.all_gather(node_grad, 'rep', axis=0, tiled=True)  40.2 us
    reduce_scatter x1, waiting for transfers between devices, shards(): lax.psum_scatter(summed.reshape(-1, width), 'rep', scatter_dimension=0, t...  20.5 us
    unnamed x27, local copies, waits for them, and re-layouts  16.9 us
    unnamed x1, blocking collectives  16.9 us
  transfers between devices with their start and end apart: 5, of which 5 were waited for; matrix products, arithmetic and copies ran while one was open for 1% of the time, Pallas kernels for 1%

profile of v1, /device:TPU:8, one launch (start us, length us, event | category | flops | bytes accessed | tf_op | source)
XLA Modules:
  0.0 625.0 jit_solution(5569512861820740546)
XLA Ops:
  7.2 0.0 copy-start
  7.2 0.0 all-gather.6.cloned.1.call-start
  7.2 0.7 all-gather.6.cloned.1.call-update
  7.9 0.0 reduce-scatter.3.cloned.1.call-start
  8.0 0.8 copy.14
  8.7 0.1 reshape.28.rows_ref
  8.8 0.8 copy.15
  9.6 0.1 reshape.29.cols_ref
  9.7 90.8 %all-gather.6.cloned.1.call-done = bf16[8192,256]{1,0:T(8,128)(2,1)} async-done(((bf16[256,256]{1,0:T(8,128)(2,1)}), bf16[8192,256]{1,0:T(8,128)(2,1)}) %all-gather.6.cloned.1.call-update) | async-done | bytes 4194320 | tf_op jit(solution)/shard_map/all_gather | solution.py:54
  100.5 0.0 copy-start.2
  100.5 3.4 copy-done.2
  103.9 0.0 copy-start.5
  103.9 2.2 copy-done.5
  106.1 0.0 copy-start.7
  106.1 0.7 copy-done.7
  106.8 10.2 %shard_map.94 = (f32[16,128,256]{2,1,0:T(8,128)}, f32[16,128,1]{2,1,0:T(8,128)S(1)}, bf16[32,4,128,128]{3,2,1,0:T(8,128)(2,1)S(1)}) custom-call(s32[128]{0:T(128)S(1)} %reshape.28.rows_ref, s32[128]{0:T(128)S(1)} %reshape.29.cols_ref, s32[32]{0:T(128)S(1)} %bitcast.22, s32[32,4,128,128]{3,2,1,0:T(8,128)S(1)} %bitcast.19, bf16[32,256,256]{2,1,0:T(8,128)(2,1)S(1)} %bitcast.20), custom_call_target="tpu_custom_call" | custom-call | tf_op jit(solution)/shard_map/pallas_call | solution.py:55
  116.9 1.9 copy-done.3
  118.9 0.0 reduce-scatter.3.cloned.1.call-update
  118.9 0.0 all-gather.4.cloned.1.call-start
  119.0 0.0 copy-done.11
  119.0 0.6 dynamic-slice
  120.2 0.3 reduce
  120.5 16.9 %all-reduce = f32[2048]{0:T(1024)S(1)} all-reduce(f32[2048]{0:T(1024)S(1)} %bitcast.23), channel_id=4, replica_groups=mesh['blk'=32,'rep'=8] {'rep'}, use_global_device_ids=true, to_apply=%region_1.0.clone | all-reduce | flops 2048 | bytes 16384
  137.4 0.1 fusion.1
  137.5 20.5 %reduce-scatter.3.cloned.1.call-done = f32[256,256]{1,0:T(8,128)} async-done(((f32[2048,256]{1,0:T(8,128)}), f32[256,256]{1,0:T(8,128)}) %reduce-scatter.3.cloned.1.call-update) | async-done | bytes 262160 | tf_op jit(solution)/shard_map/reduce_scatter | solution.py:77
  158.0 0.0 copy-done.9
  158.0 1.1 multiply_convert_fusion.2
  159.1 0.0 copy-done
  159.1 0.0 copy-done.10
  159.1 0.9 multiply_convert_fusion
  160.0 0.9 fusion
  160.9 0.0 all-gather.4.cloned.1.call-update
  160.9 0.0 all-reduce.3.cloned.1.call-start
  161.0 0.9 fusion.2
  161.9 0.0 all-reduce.3.cloned.1.call-update
  161.9 0.0 reduce-scatter.5.cloned.1.call-start
  162.0 40.2 %all-gather.4.cloned.1.call-done = bf16[2048,256]{1,0:T(8,128)(2,1)} async-done(((bf16[256,256]{1,0:T(8,128)(2,1)}), bf16[2048,256]{1,0:T(8,128)(2,1)}) %all-gather.4.cloned.1.call-update) | async-done | bytes 1048592 | tf_op jit(solution)/shard_map/all_gather | solution.py:89
  202.2 2.2 copy-done.4
  204.4 1.2 copy-done.6
  205.6 9.3 %shard_map.95 = f32[32,2,128,256]{3,2,1,0:T(8,128)S(1)} custom-call(s32[128]{0:T(128)S(1)} %reshape.28.rows_ref, s32[128]{0:T(128)S(1)} %reshape.29.cols_ref, bf16[32,4,128,128]{3,2,1,0:T(8,128)(2,1)S(1)} %copy-done.4, bf16[16,128,256]{2,1,0:T(8,128)(2,1)S(1)} %bitcast.21), custom_call_target="tpu_custom_call" | custom-call | tf_op jit(solution)/shard_map/pallas_call | solution.py:90
  214.9 0.0 copy-start.1
  215.0 3.2 copy-done.1
  218.2 0.0 reduce-scatter.5.cloned.1.call-update
  218.2 241.5 %all-reduce.3.cloned.1.call-done = f32[256,256]{1,0:T(8,128)} async-done(((f32[256,256]{1,0:T(8,128)}), f32[256,256]{1,0:T(8,128)}) %all-reduce.3.cloned.1.call-update) | async-done | bytes 262160 | tf_op jit(solution)/shard_map/psum | solution.py:86
  459.7 1.7 broadcast_multiply_fusion
  461.4 155.5 %reduce-scatter.5.cloned.1.call-done = f32[256,256]{1,0:T(8,128)} async-done(((f32[8192,256]{1,0:T(8,128)}), f32[256,256]{1,0:T(8,128)}) %reduce-scatter.5.cloned.1.call-update) | async-done | bytes 262160 | tf_op jit(solution)/shard_map/reduce_scatter | solution.py:104
  616.9 0.0 copy-done.8
  616.9 1.6 add_convert_fusion
  (7 shorter events, 0.0 us)
Async XLA Ops:
  7.2 151.9 %copy-start = (bf16[256,256]{1,0:T(8,128)(2,1)S(1)}, bf16[256,256]{1,0:T(8,128)(2,1)}, u32[]{:S(2)}) copy-start(bf16[256,256]{1,0:T(8,128)(2,1)} %param.8) | copy-start | bytes 393220
  7.2 93.3 %all-gather.6.cloned.1.call-start = ((), (), s32[]{:S(2)}) async-start(), calls=%async_computation.6 | async-start | bytes 4325376 | tf_op jit(solution)/shard_map/all_gather | solution.py:54
  7.9 150.1 %reduce-scatter.3.cloned.1.call-start = ((), (), s32[]{:S(2)}) async-start(), calls=%async_computation.2 | async-start | bytes 2359296 | tf_op jit(solution)/shard_map/reduce_scatter | solution.py:77
  100.5 3.4 copy-start.2
  103.9 2.2 copy-start.5
  106.1 0.7 copy-start.7
  106.7 12.2 %copy-start.11 = (u32[256]{0:T(256)S(1)}, u32[256]{0:T(256)}, u32[]{:S(2)}) copy-start(u32[256]{0:T(256)} %constant.11) | copy-start | bytes 3076
  106.7 51.2 %copy-start.9 = (bf16[256,256]{1,0:T(8,128)(2,1)S(1)}, bf16[256,256]{1,0:T(8,128)(2,1)}, u32[]{:S(2)}) copy-start(bf16[256,256]{1,0:T(8,128)(2,1)} %param.7) | copy-start | bytes 393220
  106.7 52.3 %copy-start.10 = (bf16[256,256]{1,0:T(8,128)(2,1)S(1)}, bf16[256,256]{1,0:T(8,128)(2,1)}, u32[]{:S(2)}) copy-start(bf16[256,256]{1,0:T(8,128)(2,1)} %param.9) | copy-start | bytes 393220
  116.9 1.9 copy-start.3
  118.9 83.3 %all-gather.4.cloned.1.call-start = ((), (), s32[]{:S(2)}) async-start(), calls=%async_computation.3 | async-start | bytes 1179648 | tf_op jit(solution)/shard_map/all_gather | solution.py:89
  160.9 298.8 %all-reduce.3.cloned.1.call-start = ((), (), s32[]{:S(2)}) async-start(), calls=%async_computation.5 | async-start | bytes 524288 | tf_op jit(solution)/shard_map/psum | solution.py:86
  161.9 455.0 %reduce-scatter.5.cloned.1.call-start = ((), (), s32[]{:S(2)}) async-start(), calls=%async_computation.4 | async-start | bytes 8650752 | tf_op jit(solution)/shard_map/reduce_scatter | solution.py:104
  202.2 2.2 copy-start.4
  204.4 1.2 copy-start.6
  214.9 3.2 copy-start.1
  218.2 398.7 %copy-start.8 = (bf16[256,256]{1,0:T(8,128)(2,1)S(1)}, bf16[256,256]{1,0:T(8,128)(2,1)}, u32[]{:S(2)}) copy-start(bf16[256,256]{1,0:T(8,128)(2,1)} %fusion) | copy-start | bytes 393220
Sparse Core Ops, SparseCore 0:
  10.8 89.6 all-gather.5
  119.0 38.9 reduce-scatter.2
  161.0 41.1 all-gather.3
  208.1 251.5 all-reduce.2
  463.9 152.8 reduce-scatter.4

commit v2 on v1

v2 whole, which is shorter than its diff:
```python
import jax
import jax.numpy as jnp
from jax import lax
from jax.experimental import pallas as pl
from jax.experimental.pallas import tpu as pltpu
from jax.sharding import PartitionSpec as P

TILE = 128
SLOT = 4
MESH = pl.DeviceIdType.MESH
F32 = jnp.float32
BF16 = jnp.bfloat16
NZ, NBLK, NREP, NX = 8, 32, 8, 2
POS = NBLK * SLOT


def rem(a, n):
    return lax.rem(a, jnp.int32(n))


def div(a, n):
    return lax.div(a, jnp.int32(n))


def loop(lo, hi, body):
    lax.fori_loop(lo, hi, lambda i, _: (body(i), 0)[1], 0)


def layer_kernel(
    rows_ref, cols_ref, count_ref, rowsv_ref, x_hbm, w_hbm, ct_hbm, tiles_hbm,
    act_ref, fgrad_ref, wgrad_ref,
    xbuf, dbuf, stage, sbuf, degs, idxv, idxs, wbuf, ctbuf,
    rs_src, rs_dst, own, deg_src, deg_dst, mixed, ngt, gt0, gt1,
    ss, sr, zs, zr, xs, xr,
    wp_src, wp_dst, w2s, w2r, w3s, w3r, w4s, w4r, w5s, w5r, w6s, w6r,
    in_sem, tile_sem, idx_sem,
    x_recv, xr_send, xl_send, xs_send, xx_send,
    rs_send, rs_recv, dg_send, dg_recv, g_send, g_recv,
    ss_send, ss_recv, z_send, z_recv, xf_send, xf_recv,
    w1_send, w1_recv, w23_send, w23_recv, w4_send, w4_recv, w5_send, w5_recv, w6_send, w6_recv,
):
    b = lax.axis_index("blk")
    rep = lax.axis_index("rep")
    z, xh, c = div(b, 4), rem(div(b, 2), 2), rem(b, 2)
    gts = (gt0, gt1)

    def blkidx(dz, xq, cq):
        return rem(z + dz + 8, 8) * 4 + rem(xh + xq, 2) * 2 + rem(c + cq, 2)

    def zdev(dz):
        return (blkidx(dz, 0, 0), rep)

    right, left = zdev(1), zdev(-1)
    sibling = (blkidx(0, 0, 1), rep)
    xmate = (blkidx(0, 1, 0), rep)

    def repdev(i):
        return (b, rem(rep + i, NREP))

    def remote(src, dst, send, recv, dev):
        return pltpu.make_async_remote_copy(
            src_ref=src, dst_ref=dst, send_sem=send, recv_sem=recv, device_id=dev, device_id_type=MESH)

    def own_load(h):
        return pltpu.make_async_copy(x_hbm.at[:, pl.ds(h * TILE, TILE)], xbuf.at[h, b], in_sem.at[h])

    def tile_load(p):
        zi, q = div(p, 4), rem(p, 4)
        return pltpu.make_async_copy(tiles_hbm.at[group_at(zi, q)], stage.at[p], tile_sem.at[p])

    def group_at(zi, q):
        odd = rem(zi, 2)
        dz = div(zi, 2) * (1 - 2 * odd) - odd
        return blkidx(dz, div(q, 2), rem(q, 2))

    w_load = pltpu.make_async_copy(w_hbm, wbuf, in_sem.at[2])
    ct_load = pltpu.make_async_copy(ct_hbm, ctbuf, in_sem.at[3])
    idx_copy = pltpu.make_async_copy(idxv, idxs, idx_sem)
    own_load(0).start()
    own_load(1).start()
    loop(0, NBLK, lambda p: tile_load(p).start())
    w_load.start()
    ct_load.start()

    bar = pltpu.get_barrier_semaphore()
    for dev in (sibling, xmate):
        pl.semaphore_signal(bar, inc=1, device_id=dev, device_id_type=MESH)
    loop(1, NZ, lambda i: pl.semaphore_signal(bar, inc=1, device_id=zdev(i), device_id_type=MESH))
    loop(1, NREP, lambda i: pl.semaphore_signal(bar, inc=1, device_id=repdev(i), device_id_type=MESH))

    def rank(i):
        s, j = i & 3, i >> 2
        cj, xj, zj = j & 1, (j >> 1) & 1, j >> 2
        dz = (zj - z + 8) & 7
        zi = jnp.where(dz < 4, 2 * dz, 15 - 2 * dz)
        q = ((xj + xh) & 1) * 2 + ((cj + c) & 1)
        return (zi * 4 + q) * 4 + s

    sub = lax.broadcasted_iota(jnp.int32, (POS, POS), 0)
    lane = lax.broadcasted_iota(jnp.int32, (POS, POS), 1)
    row_l = jnp.broadcast_to(rowsv_ref[...], (POS, POS))
    row_s = jnp.transpose(row_l)
    rank_s, rank_l = rank(sub), rank(lane)
    prev = jnp.max(jnp.where((row_l == row_s) & (rank_s < rank_l), rank_s, -1), axis=0, keepdims=True)
    last = jnp.max(jnp.where(row_s == lane, rank_s, -1), axis=0, keepdims=True)
    idxv[0:1, :] = jnp.where(prev < 0, POS, prev)
    idxv[1:2, :] = jnp.where(last < 0, POS, last)
    idxv[2:8, :] = jnp.zeros((6, POS), jnp.int32)
    idx_copy.start()
    sbuf[POS] = jnp.zeros((TILE, TILE), F32)
    degs[POS] = jnp.zeros((8, TILE), F32)

    own_load(0).wait()
    own_load(1).wait()
    pl.semaphore_wait(bar, 16)

    def f_right(h, j):
        return remote(xbuf.at[h, j], xbuf.at[h, j], xr_send.at[h, j], x_recv.at[h, j], right)

    def f_left(h, j):
        return remote(xbuf.at[h, j], xbuf.at[h, j], xl_send.at[h, j], x_recv.at[h, j], left)

    def f_sib(h, j):
        return remote(xbuf.at[h, j], xbuf.at[h, j], xs_send.at[h, j], x_recv.at[h, j], sibling)

    def f_mate(h):
        return remote(xbuf.at[h, b], xbuf.at[h, b], xx_send.at[h], x_recv.at[h, b], xmate)

    def f_wait(h, j):
        f_sib(h, j).wait_recv()

    def start_own(h):
        f_mate(h).start()
        f_right(h, b).start()
        f_left(h, b).start()
        f_sib(h, b).start()

    start_own(0)
    idx_copy.wait()

    def prep(p, j):
        tile_load(p).wait()
        for s in range(SLOT):
            live = s < count_ref[j]
            col = cols_ref[j * SLOT + s]
            m0 = jnp.where(live & (col == 0), 1.0, 0.0).astype(F32)
            m1 = jnp.where(live & (col == 1), 1.0, 0.0).astype(F32)
            tile = stage[p, s].astype(F32)
            dbuf[j, pl.ds(s * TILE, TILE), 0:TILE] = (tile * m0).astype(BF16)
            dbuf[j, pl.ds(s * TILE, TILE), TILE:2 * TILE] = (tile * m1).astype(BF16)
        ones = jnp.ones((16, 2 * TILE), BF16)
        sums = lax.dot_general(ones, dbuf[j], (((1,), (1,)), ((), ())), preferred_element_type=F32)
        for s in range(SLOT):
            degs[p * SLOT + s] = sums[0:8, s * TILE:(s + 1) * TILE] + degs[idxs[0, j * SLOT + s]]

    def process(h, p):
        zi, q = div(p, 4), rem(p, 4)
        j = group_at(zi, q)
        pl.when(rem(q, 2) == 1)(lambda: f_wait(h, j))
        if h == 0:
            prep(p, j)
        prod = jnp.dot(dbuf[j], xbuf[h, j], preferred_element_type=F32)
        for s in range(SLOT):
            sbuf[p * SLOT + s] = prod[s * TILE:(s + 1) * TILE] + sbuf[idxs[0, j * SLOT + s]]

    def rs_copy(h, r):
        return remote(rs_src.at[h, r], rs_dst.at[h, rep], rs_send.at[h, r], rs_recv.at[h, rep], (b, r))

    def rs_arrival(h, r):
        return remote(rs_src.at[h, r], rs_dst.at[h, r], rs_send.at[h, r], rs_recv.at[h, r], (b, r))

    def dg_copy(r):
        return remote(deg_src.at[r], deg_dst.at[rep], dg_send.at[r], dg_recv.at[rep], (b, r))

    def dg_arrival(r):
        return remote(deg_src.at[r], deg_dst.at[r], dg_send.at[r], dg_recv.at[r], (b, r))

    def forward_half(h):
        far_r, far_l = 4 - h, 3 + h
        jx = blkidx(0, 1, 0)
        f_wait(h, jx)
        f_right(h, jx).start()
        f_left(h, jx).start()
        f_sib(h, jx).start()

        def event(e):
            k, v = 1 + div(e, 4), rem(e, 4)
            sgn, xq = rem(v, 2), div(v, 2)
            j = blkidx(k * (2 * sgn - 1), xq, 0)
            f_wait(h, j)
            pl.when((sgn == 0) & (k < far_r))(lambda: f_right(h, j).start())
            pl.when((sgn == 1) & (k < far_l))(lambda: f_left(h, j).start())
            f_sib(h, j).start()
            p0 = jnp.where(k == 1, v, 4 + (k - 2) * 8 + v * 2)
            loop(p0, p0 + jnp.where(k == 1, 1, 2), lambda p: process(h, p))

        loop(0, 12, event)
        if h == 0:
            start_own(1)

        def far(xq):
            j = blkidx(4, xq, 0)
            f_wait(h, j)
            f_sib(h, j).start()
            loop(20 + xq * 4, 24 + xq * 4, lambda p: process(h, p))

        loop(0, 2, far)
        loop(28, 32, lambda p: process(h, p))

        def chunk(i):
            r = rem(rep + i, NREP)
            for t in range(2):
                rs_src[h, r, pl.ds(t * TILE, TILE)] = sbuf[idxs[1, 2 * r + t]].astype(BF16)
            rs_copy(h, r).start()
            if h == 0:
                for t in range(2):
                    deg_src[r, t] = degs[idxs[1, 2 * r + t]]
                dg_copy(r).start()

        loop(1, NREP, chunk)
        for t in range(2):
            own[h, pl.ds(t * TILE, TILE)] = sbuf[idxs[1, 2 * rep + t]]
            if h == 0:
                deg_src[rep, t] = degs[idxs[1, 2 * rep + t]]

    forward_half(0)
    forward_half(1)

    w_load.wait()
    ct_load.wait()
    loop(1, NREP, lambda i: dg_arrival(rem(rep + i, NREP)).wait_recv())
    deg = deg_src[rep]
    for i in range(1, NREP):
        deg = deg + deg_dst[rem(rep + i, NREP)]
    scale = lax.rsqrt(deg + 1.0)
    scale_row = jnp.concatenate([scale[0, 0:1], scale[1, 0:1]], axis=1)
    scale_col = [jnp.transpose(jnp.broadcast_to(scale[t, 0:1], (TILE, TILE))) for t in range(2)]
    for h in range(2):
        def add(i):
            r = rem(rep + i, NREP)
            rs_arrival(h, r).wait_recv()
            own[h] += rs_dst[h, r].astype(F32)

        loop(1, NREP, add)
        for t in range(2):
            part = own[h, pl.ds(t * TILE, TILE)] + xbuf[h, b, pl.ds(t * TILE, TILE)].astype(F32)
            mixed[pl.ds(t * TILE, TILE), h * TILE:(h + 1) * TILE] = (part * scale_col[t]).astype(BF16)
    pre = jnp.dot(mixed[...], wbuf[...], preferred_element_type=F32)
    sig = 1.0 / (1.0 + jnp.exp(-pre))
    act_ref[...] = (pre * sig).astype(BF16)
    act_grad = (ctbuf[...].astype(F32) * sig * (1.0 + pre * (1.0 - sig))).astype(BF16)

    def g_copy(h, i):
        mine = gts[h].at[pl.ds(2 * rep, 2)]
        return remote(mine, mine, g_send.at[h, i], g_recv.at[h, rep], repdev(i))

    def g_arrival(h, r):
        part = gts[h].at[pl.ds(2 * r, 2)]
        return remote(part, part, g_send.at[h, 0], g_recv.at[h, r], (b, r))

    for h in range(2):
        back = lax.dot_general(
            wbuf[h * TILE:(h + 1) * TILE, :], act_grad, (((1,), (1,)), ((), ())), preferred_element_type=F32)
        grad = (back * scale_row).astype(BF16)
        ngt[h] = grad
        for t in range(2):
            gts[h][2 * rep + t] = grad[:, t * TILE:(t + 1) * TILE]
        loop(1, NREP, lambda i: g_copy(h, i).start())

    def w1_copy(r):
        return remote(wp_src.at[r], wp_dst.at[rep], w1_send.at[r], w1_recv.at[rep], (b, r))

    def w1_arrival(r):
        return remote(wp_src.at[r], wp_dst.at[r], w1_send.at[r], w1_recv.at[r], (b, r))

    w2_copy = remote(w2s, w2r, w23_send.at[0], w23_recv.at[0], sibling)
    w3_copy = remote(w3s, w3r, w23_send.at[1], w23_recv.at[1], xmate)

    def w4_copy(i):
        zz = rem(z + i, NZ)
        return remote(w4s.at[zz], w4r.at[z], w4_send.at[zz], w4_recv.at[z], zdev(i))

    def w4_arrival(zz):
        return remote(w4s.at[zz], w4r.at[zz], w4_send.at[zz], w4_recv.at[zz], right)

    def w5_copy(i):
        return remote(w5s, w5r.at[z], w5_send.at[i], w5_recv.at[z], zdev(i))

    def w5_arrival(zz):
        return remote(w5s, w5r.at[zz], w5_send.at[0], w5_recv.at[zz], right)

    def w6_copy(i):
        return remote(w6s, w6r.at[rep], w6_send.at[i], w6_recv.at[rep], repdev(i))

    def w6_arrival(r):
        return remote(w6s, w6r.at[r], w6_send.at[0], w6_recv.at[r], (b, r))

    part = lax.dot_general(mixed[...], act_grad, (((0,), (0,)), ((), ())), preferred_element_type=F32)
    for r in range(NREP):
        wp_src[r] = part[r * 32:(r + 1) * 32]
    loop(1, NREP, lambda i: w1_copy(rem(rep + i, NREP)).start())

    def w_step2():
        loop(1, NREP, lambda i: w1_arrival(rem(rep + i, NREP)).wait_recv())
        wp_dst[rep] = wp_src[rep]
        w2s[...] = sum(wp_dst[r] for r in range(NREP))
        w2_copy.start()

    def w_step3():
        w2_copy.wait_recv()
        w3s[...] = w2s[...] + w2r[...]
        w3_copy.start()

    def w_step4():
        w3_copy.wait_recv()
        both = w3s[...] + w3r[...]
        for k in range(NZ):
            w4s[k] = both[(k // 2) * 8:(k // 2) * 8 + 8, (k % 2) * TILE:(k % 2) * TILE + TILE]
        loop(1, NZ, lambda i: w4_copy(i).start())

    def w_step5():
        loop(1, NZ, lambda i: w4_arrival(rem(z + i, NZ)).wait_recv())
        w4r[z] = w4s[z]
        w5s[...] = sum(w4r[k] for k in range(NZ))
        loop(1, NZ, lambda i: w5_copy(i).start())

    def w_step6():
        loop(1, NZ, lambda i: w5_arrival(rem(z + i, NZ)).wait_recv())
        w5r[z] = w5s[...]
        for k in range(NZ):
            w6s[(k // 2) * 8:(k // 2) * 8 + 8, (k % 2) * TILE:(k % 2) * TILE + TILE] = w5r[k]
        loop(1, NREP, lambda i: w6_copy(i).start())

    def w_step7():
        loop(1, NREP, lambda i: w6_arrival(rem(rep + i, NREP)).wait_recv())
        w6r[rep] = w6s[...]
        for r in range(NREP):
            wgrad_ref[r * 32:(r + 1) * 32] = w6r[r] * (NBLK * NREP * 2 * TILE) ** -0.5

    def out_t(h, j):
        left_side = jnp.concatenate([gts[h][rows_ref[j * SLOT + s]] for s in range(SLOT)], axis=1)
        return jnp.dot(left_side, dbuf[j], preferred_element_type=F32)

    def sib_copy(h, k):
        return remote(ss.at[h, k], sr.at[h, k], ss_send.at[h, k], ss_recv.at[h, k], sibling)

    def z_copy(h, d, m, xq):
        i = (d * 4 + m - 1) * 2 + xq
        dev = (jnp.where(d == 0, right[0], left[0]), rep)
        return remote(zs.at[h, i], zr.at[h, i], z_send.at[h, i], z_recv.at[h, i], dev)

    def z_arrival(h, d, m, xq):
        i = (d * 4 + m) * 2 + xq
        return remote(zs.at[h, i], zr.at[h, i], z_send.at[h, i], z_recv.at[h, i], right)

    def z_value(h, d, m, xq):
        return zr[h, (d * 4 + m) * 2 + xq].astype(F32)

    def x_copy(h):
        return remote(xs.at[h], xr.at[h], xf_send.at[h], xf_recv.at[h], xmate)

    def sib_term(h, d, m, xq):
        dz = m * (1 - 2 * d)
        k = rem(dz + 8, 8) * 2 + xq
        ss[h, k] = out_t(h, blkidx(dz, xq, 1)).astype(BF16)
        sib_copy(h, k).start()

    def own_term(h, d, m, xq, first):
        dz = m * (1 - 2 * d)
        k = rem(dz + 8, 8) * 2 + xq
        value = out_t(h, blkidx(dz, xq, 0))
        sib_copy(h, k).wait_recv()
        value = value + sr[h, k].astype(F32)
        if not first:
            return value, k
        zs[h, (d * 4 + m - 1) * 2 + xq] = value.astype(BF16)
        z_copy(h, d, m, xq).start()

    def pass_on(h, d, m, xq):
        value, _ = own_term(h, d, m, xq, False)
        i = (d * 4 + m) * 2 + xq
        z_arrival(h, d, m, xq).wait_recv()
        zs[h, i - 2] = (value + zr[h, i].astype(F32)).astype(BF16)
        z_copy(h, d, m, xq).start()

    def backward_open(h):
        long, short = h, 1 - h
        loop(1, NREP, lambda i: g_arrival(h, rem(rep + i, NREP)).wait_recv())
        loop(0, 2, lambda q: sib_term(h, long, 4, q))
        loop(0, 2, lambda q: sib_term(h, short, 3, q))
        loop(0, 2, lambda q: own_term(h, long, 4, q, True))
        loop(0, 2, lambda q: sib_term(h, long, 3, q))
        loop(0, 2, lambda q: own_term(h, short, 3, q, True))

    def backward_mid(h):
        long, short = h, 1 - h

        def third(q):
            sib_term(h, 0, 2, q)
            sib_term(h, 1, 2, q)
            pass_on(h, long, 3, q)

        loop(0, 2, third)

        def second(e):
            d, q = rem(e, 2), div(e, 2)
            sib_term(h, d, 1, q)
            pass_on(h, d, 2, q)

        loop(0, 4, second)
        loop(0, 2, lambda q: sib_term(h, 0, 0, q))
        loop(0, 4, lambda e: pass_on(h, rem(e, 2), 1, div(e, 2)))

    def settled(h, xq):
        value, _ = own_term(h, 0, 0, xq, False)
        z_arrival(h, 0, 0, xq).wait_recv()
        z_arrival(h, 1, 0, xq).wait_recv()
        return value + z_value(h, 0, 0, xq) + z_value(h, 1, 0, xq)

    def to_mate(h):
        xs[h] = settled(h, 1).astype(BF16)
        x_copy(h).start()

    def finish(h):
        value = settled(h, 0)
        x_copy(h).wait_recv()
        value = value + xr[h].astype(F32) + ngt[h].astype(F32)
        fgrad_ref[:, h * TILE:(h + 1) * TILE] = jnp.transpose(value).astype(BF16)

    backward_open(0)
    w_step2()
    backward_mid(0)
    w_step3()
    backward_open(1)
    w_step4()
    to_mate(0)
    w_step5()
    backward_mid(1)
    w_step6()
    finish(0)
    to_mate(1)
    w_step7()
    finish(1)

    for h in range(2):
        far_r, far_l = 4 - h, 3 + h
        f_mate(h).wait_send()

        def drain_f(e):
            k, xq = div(e, 2), rem(e, 2)
            f_right(h, blkidx(-k, xq, 0)).wait_send()
            f_left(h, blkidx(k, xq, 0)).wait_send()

        loop(0, 6, drain_f)

        def drain_long(xq):
            if h == 0:
                f_right(h, blkidx(-3, xq, 0)).wait_send()
            else:
                f_left(h, blkidx(3, xq, 0)).wait_send()
            z_copy(h, h, 4, xq).wait_send()

        loop(0, 2, drain_long)

        def drain_s(e):
            f_sib(h, blkidx(div(e, 2), rem(e, 2), 0)).wait_send()
            sib_copy(h, e).wait_send()

        loop(0, 16, drain_s)

        def drain_z(e):
            z_copy(h, rem(e, 2), 1 + div(e, 4), rem(div(e, 2), 2)).wait_send()

        loop(0, 12, drain_z)
        x_copy(h).wait_send()

        def drain_rep(i):
            rs_copy(h, rem(rep + i, NREP)).wait_send()
            g_copy(h, i).wait_send()

        loop(1, NREP, drain_rep)

    def drain_w(i):
        r = rem(rep + i, NREP)
        dg_copy(r).wait_send()
        w1_copy(r).wait_send()
        w4_copy(i).wait_send()
        w5_copy(i).wait_send()
        w6_copy(i).wait_send()

    loop(1, NREP, drain_w)
    w2_copy.wait_send()
    w3_copy.wait_send()


def shards(node_features, weight, cotangent, tile_values, tile_rows, tile_cols, tile_count):
    half, width = TILE, 2 * TILE
    dma = pltpu.SemaphoreType.DMA
    vmem = pltpu.VMEM
    smem_spec = pl.BlockSpec(memory_space=pltpu.SMEM)
    vmem_spec = pl.BlockSpec(memory_space=pltpu.VMEM)
    any_spec = pl.BlockSpec(memory_space=pl.ANY)
    return pl.pallas_call(
        layer_kernel,
        out_shape=[
            jax.ShapeDtypeStruct((width, width), BF16),
            jax.ShapeDtypeStruct((width, width), BF16),
            jax.ShapeDtypeStruct((width, width), F32),
        ],
        in_specs=[smem_spec] * 3 + [vmem_spec] + [any_spec] * 4,
        out_specs=[vmem_spec] * 3,
        scratch_shapes=[
            vmem((2, NBLK, width, half), BF16),
            vmem((NBLK, SLOT * TILE, width), BF16),
            vmem((NBLK, SLOT, TILE, TILE), jnp.int32),
            vmem((POS + 1, TILE, TILE), F32),
            vmem((POS + 1, 8, TILE), F32),
            vmem((8, POS), jnp.int32),
            pltpu.SMEM((8, POS), jnp.int32),
            vmem((width, width), BF16),
            vmem((width, width), BF16),
            vmem((2, NREP, width, half), BF16),
            vmem((2, NREP, width, half), BF16),
            vmem((2, width, half), F32),
            vmem((NREP, 2, 8, TILE), F32),
            vmem((NREP, 2, 8, TILE), F32),
            vmem((width, width), BF16),
            vmem((2, half, width), BF16),
            vmem((2 * NREP, half, TILE), BF16),
            vmem((2 * NREP, half, TILE), BF16),
            vmem((2, 16, half, width), BF16),
            vmem((2, 16, half, width), BF16),
            vmem((2, 16, half, width), BF16),
            vmem((2, 16, half, width), BF16),
            vmem((2, half, width), BF16),
            vmem((2, half, width), BF16),
            vmem((NREP, 32, width), F32),
            vmem((NREP, 32, width), F32),
            vmem((32, width), F32),
            vmem((32, width), F32),
            vmem((32, width), F32),
            vmem((32, width), F32),
            vmem((NZ, 8, TILE), F32),
            vmem((NZ, 8, TILE), F32),
            vmem((8, TILE), F32),
            vmem((NZ, 8, TILE), F32),
            vmem((32, width), F32),
            vmem((NREP, 32, width), F32),
            dma((4,)), dma((NBLK,)), dma,
            dma((2, NBLK)), dma((2, NBLK)), dma((2, NBLK)), dma((2, NBLK)), dma((2,)),
            dma((2, NREP)), dma((2, NREP)), dma((NREP,)), dma((NREP,)), dma((2, NREP)), dma((2, NREP)),
            dma((2, 16)), dma((2, 16)), dma((2, 16)), dma((2, 16)), dma((2,)), dma((2,)),
            dma((NREP,)), dma((NREP,)), dma((2,)), dma((2,)), dma((NZ,)), dma((NZ,)), dma((NZ,)), dma((NZ,)),
            dma((NREP,)), dma((NREP,)),
        ],
        compiler_params=pltpu.CompilerParams(
            collective_id=0, has_side_effects=True, vmem_limit_bytes=56 << 20),
        cost_estimate=pl.CostEstimate(flops=4 << 30, bytes_accessed=9 << 20, transcendentals=1 << 16),
        name="graph_layer",
    )(
        tile_rows.reshape(-1), tile_cols.reshape(-1), tile_count.reshape(-1), tile_rows.reshape(1, -1),
        node_features, weight, cotangent, tile_values[0, 0],
    )


def solution(mesh):
    in_specs = (
        P(("blk", "rep"), None),
        P(),
        P(("blk", "rep"), None),
        P("blk", "rep", None, None, None, None),
        P("blk", "rep", None, None),
        P("blk", "rep", None, None),
        P("blk", "rep", None),
    )
    out_specs = (P(("blk", "rep"), None), P(("blk", "rep"), None), P())
    return jax.shard_map(shards, mesh=mesh, in_specs=in_specs, out_specs=out_specs, check_vma=False)
```

time: 625 us -> 127 us (0.20)
  waiting for transfers between devices: 549 us -> 0 us
  Pallas kernels: 19.5 us -> 117 us
  blocking collectives: 16.9 us -> 0 us
  between operations: 14.5 us -> 0.64 us
  local copies, waits for them, and re-layouts: 17.1 us -> 8.18 us
    psum x1 -> x0, waiting for transfers between devices: 242 us -> none  [shards(): weight_grad = lax.psum(weight_part, ('blk', 'rep')) * n_nodes ** (-0.5)]
    reduce_scatter x2 -> x0, waiting for transfers between devices: 176 us -> none  [the longest x1 156 us: shards(): lax.psum_scatter(terms.reshape(-1, width), 'blk', scatter_dimension=0, ti...]
    all_gather x2 -> x0, waiting for transfers between devices: 131 us -> none  [the longest x1 90.8 us: shards(): feats = lax.all_gather(node_features, 'blk', axis=0, tiled=False)]
    pallas_call x2 -> x1, Pallas kernels: 19.5 us -> 117 us  [shards(): pl.pallas_call(layer_kernel, out_shape=[jax.ShapeDtypeStruct((width, widt...]
    unnamed x1 -> x0, blocking collectives: 16.9 us -> none
    unnamed x27 -> x5, local copies, waits for them, and re-layouts: 16.9 us -> 6.33 us
  transfers between devices with their start and end apart: 5 -> 0, of which waited for: 5 -> 0; matrix products, arithmetic and copies ran while one was open for 1% -> 0% of each run, Pallas kernels for 1% -> 0%
where the time goes in v2:
time: 127 us; the launch traced here: 126 us
  Pallas kernels  117 us (92%)
  local copies, waits for them, and re-layouts  8.18 us (6%)
    pallas_call x1, Pallas kernels, shards(): pl.pallas_call(layer_kernel, out_shape=[jax.ShapeDtypeStruct((width, widt...  117 us
    unnamed x5, local copies, waits for them, and re-layouts  6.33 us

profile of v2, /device:TPU:8, one launch (start us, length us, event | category | flops | bytes accessed | tf_op | source)
XLA Modules:
  0.0 126.2 jit_solution(14693830584287162291)
XLA Ops:
  0.6 0.8 copy.13
  1.4 0.6 reshape.21.rowsv_ref
  2.0 0.6 reshape.18.rows_ref
  2.6 0.8 copy.14
  3.4 0.6 reshape.19.cols_ref
  4.0 117.4 %graph_layer.1 = (bf16[256,256]{1,0:T(8,128)(2,1)}, bf16[256,256]{1,0:T(8,128)(2,1)}, f32[256,256]{1,0:T(8,128)}) custom-call(s32[128]{0:T(128)} %reshape.18.rows_ref, s32[128]{0:T(128)} %reshape.19.cols_ref, s32[32]{0:T(128)} %bitcast.9, s32[1,128]{1,0:T(1,128)} %reshape.21.rowsv_ref, bf16[256,256]{1,0:T(8,128)(2,1)} %x_hbm.1, bf16[256,256]{1,0:T(8,128)(2,1)} %w_hbm.1, ...), custom_call_target="tpu_custom_call" | custom-call | flops 4294967296 | bytes 9437184 | tf_op jit(solution)/shard_map/graph_layer/pallas_call | solution.py:503
  121.4 1.6 %copy.19 = bf16[256,256]{1,0:T(8,128)(2,1)} copy(bf16[256,256]{1,0:T(8,128)(2,1)} %get-tuple-element.6) | data formatting | bytes 262144
  122.9 1.6 %copy.20 = bf16[256,256]{1,0:T(8,128)(2,1)} copy(bf16[256,256]{1,0:T(8,128)(2,1)} %get-tuple-element.7) | data formatting | bytes 262144
  124.5 1.7 %copy.21 = f32[256,256]{1,0:T(8,128)} copy(f32[256,256]{1,0:T(8,128)} %get-tuple-element.8) | data formatting | bytes 524288

commit v3 on v2

--- a/solution.py
+++ b/solution.py
@@ -88,26 +88,35 @@
     loop(1, NZ, lambda i: pl.semaphore_signal(bar, inc=1, device_id=zdev(i), device_id_type=MESH))
     loop(1, NREP, lambda i: pl.semaphore_signal(bar, inc=1, device_id=repdev(i), device_id_type=MESH))
 
-    def rank(i):
-        s, j = i & 3, i >> 2
+    def first_pos(j):
         cj, xj, zj = j & 1, (j >> 1) & 1, j >> 2
         dz = (zj - z + 8) & 7
         zi = jnp.where(dz < 4, 2 * dz, 15 - 2 * dz)
         q = ((xj + xh) & 1) * 2 + ((cj + c) & 1)
-        return (zi * 4 + q) * 4 + s
-
-    sub = lax.broadcasted_iota(jnp.int32, (POS, POS), 0)
-    lane = lax.broadcasted_iota(jnp.int32, (POS, POS), 1)
-    row_l = jnp.broadcast_to(rowsv_ref[...], (POS, POS))
-    row_s = jnp.transpose(row_l)
-    rank_s, rank_l = rank(sub), rank(lane)
-    prev = jnp.max(jnp.where((row_l == row_s) & (rank_s < rank_l), rank_s, -1), axis=0, keepdims=True)
-    last = jnp.max(jnp.where(row_s == lane, rank_s, -1), axis=0, keepdims=True)
-    idxv[0:1, :] = jnp.where(prev < 0, POS, prev)
-    idxv[1:2, :] = jnp.where(last < 0, POS, last)
-    idxv[2:8, :] = jnp.zeros((6, POS), jnp.int32)
+        return (zi * 4 + q) * SLOT
+
+    idxv[...] = jnp.zeros((8, TILE), jnp.int32)
+    idxv[0:SLOT, 0:NBLK] = rowsv_ref[...]
+    group = lax.broadcasted_iota(jnp.int32, (NBLK, TILE), 0)
+    lane = lax.broadcasted_iota(jnp.int32, (NBLK, TILE), 1)
+    group_pos, lane_pos = first_pos(group), first_pos(lane & (NBLK - 1))
+    row_l = [jnp.broadcast_to(idxv[s:s + 1, :], (TILE, TILE)) for s in range(SLOT)]
+    row_s = [jnp.transpose(row)[0:NBLK] for row in row_l]
+    last = jnp.full((NBLK, TILE), -1, jnp.int32)
+    for t in range(SLOT):
+        last = jnp.maximum(last, jnp.where(row_s[t] == lane, group_pos + t, -1))
+    last = jnp.max(last, axis=0, keepdims=True)
+    for s in range(SLOT):
+        prev = jnp.full((NBLK, TILE), -1, jnp.int32)
+        for t in range(SLOT):
+            before = (row_s[t] == row_l[s][0:NBLK]) & (group_pos + t < lane_pos + s)
+            prev = jnp.maximum(prev, jnp.where(before, group_pos + t, -1))
+        prev = jnp.max(prev, axis=0, keepdims=True)
+        idxv[s:s + 1, :] = jnp.where(prev < 0, POS, prev)
+    idxv[SLOT:SLOT + 1, :] = jnp.where(last < 0, POS, last)
     idx_copy.start()
-    sbuf[POS] = jnp.zeros((TILE, TILE), F32)
+    for h in range(2):
+        sbuf[h, POS] = jnp.zeros((TILE, TILE), F32)
     degs[POS] = jnp.zeros((8, TILE), F32)
 
     own_load(0).wait()
@@ -136,13 +145,14 @@
         f_sib(h, b).start()
 
     start_own(0)
+    start_own(1)
     idx_copy.wait()
 
     def prep(p, j):
         tile_load(p).wait()
         for s in range(SLOT):
             live = s < count_ref[j]
-            col = cols_ref[j * SLOT + s]
+            col = cols_ref[s, j]
             m0 = jnp.where(live & (col == 0), 1.0, 0.0).astype(F32)
             m1 = jnp.where(live & (col == 1), 1.0, 0.0).astype(F32)
             tile = stage[p, s].astype(F32)
@@ -151,7 +161,7 @@
         ones = jnp.ones((16, 2 * TILE), BF16)
         sums = lax.dot_general(ones, dbuf[j], (((1,), (1,)), ((), ())), preferred_element_type=F32)
         for s in range(SLOT):
-            degs[p * SLOT + s] = sums[0:8, s * TILE:(s + 1) * TILE] + degs[idxs[0, j * SLOT + s]]
+            degs[p * SLOT + s] = sums[0:8, s * TILE:(s + 1) * TILE] + degs[idxs[s, j]]
 
     def process(h, p):
         zi, q = div(p, 4), rem(p, 4)
@@ -161,7 +171,7 @@
             prep(p, j)
         prod = jnp.dot(dbuf[j], xbuf[h, j], preferred_element_type=F32)
         for s in range(SLOT):
-            sbuf[p * SLOT + s] = prod[s * TILE:(s + 1) * TILE] + sbuf[idxs[0, j * SLOT + s]]
+            sbuf[h, p * SLOT + s] = prod[s * TILE:(s + 1) * TILE] + sbuf[h, idxs[s, j]]
 
     def rs_copy(h, r):
         return remote(rs_src.at[h, r], rs_dst.at[h, rep], rs_send.at[h, r], rs_recv.at[h, rep], (b, r))
@@ -175,29 +185,32 @@
     def dg_arrival(r):
         return remote(deg_src.at[r], deg_dst.at[r], dg_send.at[r], dg_recv.at[r], (b, r))
 
-    def forward_half(h):
-        far_r, far_l = 4 - h, 3 + h
+    def forward_open(h):
         jx = blkidx(0, 1, 0)
         f_wait(h, jx)
         f_right(h, jx).start()
         f_left(h, jx).start()
         f_sib(h, jx).start()
 
-        def event(e):
-            k, v = 1 + div(e, 4), rem(e, 4)
+    def forward_step(h, k):
+        far_r, far_l = 4 - h, 3 + h
+
+        def event(v):
             sgn, xq = rem(v, 2), div(v, 2)
             j = blkidx(k * (2 * sgn - 1), xq, 0)
             f_wait(h, j)
-            pl.when((sgn == 0) & (k < far_r))(lambda: f_right(h, j).start())
-            pl.when((sgn == 1) & (k < far_l))(lambda: f_left(h, j).start())
+            if k < far_r:
+                pl.when(sgn == 0)(lambda: f_right(h, j).start())
+            if k < far_l:
+                pl.when(sgn == 1)(lambda: f_left(h, j).start())
             f_sib(h, j).start()
-            p0 = jnp.where(k == 1, v, 4 + (k - 2) * 8 + v * 2)
-            loop(p0, p0 + jnp.where(k == 1, 1, 2), lambda p: process(h, p))
-
-        loop(0, 12, event)
-        if h == 0:
-            start_own(1)
-
+            n = 1 if k == 1 else 2
+            p0 = v if k == 1 else 4 + (k - 2) * 8 + v * 2
+            loop(p0, p0 + n, lambda p: process(h, p))
+
+        loop(0, 4, event)
+
+    def forward_close(h):
         def far(xq):
             j = blkidx(4, xq, 0)
             f_wait(h, j)
@@ -210,21 +223,28 @@
         def chunk(i):
             r = rem(rep + i, NREP)
             for t in range(2):
-                rs_src[h, r, pl.ds(t * TILE, TILE)] = sbuf[idxs[1, 2 * r + t]].astype(BF16)
+                rs_src[h, r, pl.ds(t * TILE, TILE)] = sbuf[h, idxs[SLOT, 2 * r + t]].astype(BF16)
             rs_copy(h, r).start()
             if h == 0:
                 for t in range(2):
-                    deg_src[r, t] = degs[idxs[1, 2 * r + t]]
+                    deg_src[r, t] = degs[idxs[SLOT, 2 * r + t]]
                 dg_copy(r).start()
 
         loop(1, NREP, chunk)
         for t in range(2):
-            own[h, pl.ds(t * TILE, TILE)] = sbuf[idxs[1, 2 * rep + t]]
+            own[h, pl.ds(t * TILE, TILE)] = sbuf[h, idxs[SLOT, 2 * rep + t]]
             if h == 0:
-                deg_src[rep, t] = degs[idxs[1, 2 * rep + t]]
-
-    forward_half(0)
-    forward_half(1)
+                deg_src[rep, t] = degs[idxs[SLOT, 2 * rep + t]]
+
+    forward_open(0)
+    forward_open(1)
+    for k in range(1, 4):
+        forward_step(0, k)
+        if k > 1:
+            forward_step(1, k - 1)
+    forward_close(0)
+    forward_step(1, 3)
+    forward_close(1)
 
     w_load.wait()
     ct_load.wait()
@@ -338,7 +358,7 @@
             wgrad_ref[r * 32:(r + 1) * 32] = w6r[r] * (NBLK * NREP * 2 * TILE) ** -0.5
 
     def out_t(h, j):
-        left_side = jnp.concatenate([gts[h][rows_ref[j * SLOT + s]] for s in range(SLOT)], axis=1)
+        left_side = jnp.concatenate([gts[h][rows_ref[s, j]] for s in range(SLOT)], axis=1)
         return jnp.dot(left_side, dbuf[j], preferred_element_type=F32)
 
     def sib_copy(h, k):
@@ -392,22 +412,23 @@
         loop(0, 2, lambda q: sib_term(h, long, 3, q))
         loop(0, 2, lambda q: own_term(h, short, 3, q, True))
 
-    def backward_mid(h):
-        long, short = h, 1 - h
-
+    def backward_third(h):
         def third(q):
             sib_term(h, 0, 2, q)
             sib_term(h, 1, 2, q)
-            pass_on(h, long, 3, q)
+            pass_on(h, h, 3, q)
 
         loop(0, 2, third)
 
+    def backward_second(h):
         def second(e):
             d, q = rem(e, 2), div(e, 2)
             sib_term(h, d, 1, q)
             pass_on(h, d, 2, q)
 
         loop(0, 4, second)
+
+    def backward_first(h):
         loop(0, 2, lambda q: sib_term(h, 0, 0, q))
         loop(0, 4, lambda e: pass_on(h, rem(e, 2), 1, div(e, 2)))
 
@@ -429,17 +450,21 @@
 
     backward_open(0)
     w_step2()
-    backward_mid(0)
+    backward_open(1)
     w_step3()
-    backward_open(1)
+    backward_third(0)
+    backward_third(1)
     w_step4()
+    backward_second(0)
+    backward_second(1)
+    w_step5()
+    backward_first(0)
+    backward_first(1)
+    w_step6()
     to_mate(0)
-    w_step5()
-    backward_mid(1)
-    w_step6()
-    finish(0)
     to_mate(1)
     w_step7()
+    finish(0)
     finish(1)
 
     for h in range(2):
@@ -493,6 +518,12 @@
     w3_copy.wait_send()
 
 
+def place_kernel(a, b, c, out_a, out_b, out_c):
+    out_a[...] = a[...]
+    out_b[...] = b[...]
+    out_c[...] = c[...]
+
+
 def shards(node_features, weight, cotangent, tile_values, tile_rows, tile_cols, tile_count):
     half, width = TILE, 2 * TILE
     dma = pltpu.SemaphoreType.DMA
@@ -500,7 +531,8 @@
     smem_spec = pl.BlockSpec(memory_space=pltpu.SMEM)
     vmem_spec = pl.BlockSpec(memory_space=pltpu.VMEM)
     any_spec = pl.BlockSpec(memory_space=pl.ANY)
-    return pl.pallas_call(
+    rows = tile_rows[0, 0].T
+    outs = pl.pallas_call(
         layer_kernel,
         out_shape=[
             jax.ShapeDtypeStruct((width, width), BF16),
@@ -513,7 +545,7 @@
             vmem((2, NBLK, width, half), BF16),
             vmem((NBLK, SLOT * TILE, width), BF16),
             vmem((NBLK, SLOT, TILE, TILE), jnp.int32),
-            vmem((POS + 1, TILE, TILE), F32),
+            vmem((2, POS + 1, TILE, TILE), F32),
             vmem((POS + 1, 8, TILE), F32),
             vmem((8, POS), jnp.int32),
             pltpu.SMEM((8, POS), jnp.int32),
@@ -558,9 +590,16 @@
         cost_estimate=pl.CostEstimate(flops=4 << 30, bytes_accessed=9 << 20, transcendentals=1 << 16),
         name="graph_layer",
     )(
-        tile_rows.reshape(-1), tile_cols.reshape(-1), tile_count.reshape(-1), tile_rows.reshape(1, -1),
+        rows, tile_cols[0, 0].T, tile_count.reshape(-1), rows,
         node_features, weight, cotangent, tile_values[0, 0],
     )
+    return pl.pallas_call(
+        place_kernel,
+        out_shape=[jax.ShapeDtypeStruct(out.shape, out.dtype) for out in outs],
+        in_specs=[vmem_spec] * 3,
+        out_specs=[vmem_spec] * 3,
+        name="place",
+    )(*outs)
 
 
 def solution(mesh):

time: 127 us -> 106 us (0.83)
  Pallas kernels: 117 us -> 104 us
  local copies, waits for them, and re-layouts: 8.18 us -> 0 us
    pallas_call x1, Pallas kernels: 117 us -> 102 us  [shards(): pl.pallas_call(layer_kernel, out_shape=[jax.ShapeDtypeStruct((width, widt...]
    unnamed x5 -> x0, local copies, waits for them, and re-layouts: 6.33 us -> none
    pallas_call x0 -> x1, Pallas kernels: none -> 1.88 us  [shards(): pl.pallas_call(place_kernel, out_shape=[jax.ShapeDtypeStruct(out.shape, o...]
    reshape x3 -> x0, local copies, waits for them, and re-layouts: 1.85 us -> none  [the longest x1 0.62 us: shards(): tile_rows.reshape(1, -1)]
where the time goes in v3:
time: 106 us; the launch traced here: 104 us
  Pallas kernels  104 us (98%)
    pallas_call x1, Pallas kernels, shards(): pl.pallas_call(layer_kernel, out_shape=[jax.ShapeDtypeStruct((width, widt...  102 us

profile of v3, /device:TPU:8, one launch (start us, length us, event | category | flops | bytes accessed | tf_op | source)
XLA Modules:
  0.0 104.4 jit_solution(18070954842813530797)
XLA Ops:
  0.6 101.8 %graph_layer.1 = (bf16[256,256]{1,0:T(8,128)(2,1)}, bf16[256,256]{1,0:T(8,128)(2,1)}, f32[256,256]{1,0:T(8,128)}) custom-call(s32[4,32]{1,0:T(4,128)} %bitcast.9, s32[4,32]{1,0:T(4,128)} %bitcast.11, s32[32]{0:T(128)} %bitcast.12, s32[4,32]{1,0:T(4,128)} %bitcast.10, bf16[256,256]{1,0:T(8,128)(2,1)} %x_hbm.1, bf16[256,256]{1,0:T(8,128)(2,1)} %w_hbm.1, ...), custom_call_target="tpu_custom_call" | custom-call | flops 4294967296 | bytes 9437184 | tf_op jit(solution)/shard_map/graph_layer/pallas_call | solution.py:535
  102.5 1.9 %place.1 = (bf16[256,256]{1,0:T(8,128)(2,1)}, bf16[256,256]{1,0:T(8,128)(2,1)}, f32[256,256]{1,0:T(8,128)}) custom-call(bf16[256,256]{1,0:T(8,128)(2,1)} %get-tuple-element.6.a, bf16[256,256]{1,0:T(8,128)(2,1)} %get-tuple-element.7.b, f32[256,256]{1,0:T(8,128)} %get-tuple-element.8.c), custom_call_target="tpu_custom_call" | custom-call | tf_op jit(solution)/shard_map/place/pallas_call | solution.py:596

commit v4 on v3

--- a/solution.py
+++ b/solution.py
@@ -32,12 +32,12 @@
     xbuf, dbuf, stage, sbuf, degs, idxv, idxs, wbuf, ctbuf,
     rs_src, rs_dst, own, deg_src, deg_dst, mixed, ngt, gt0, gt1,
     ss, sr, zs, zr, xs, xr,
-    wp_src, wp_dst, w2s, w2r, w3s, w3r, w4s, w4r, w5s, w5r, w6s, w6r,
+    wp_src, wp_dst, w2g, w4s, w4r, w5s, w5r, w6s, w6r,
     in_sem, tile_sem, idx_sem,
     x_recv, xr_send, xl_send, xs_send, xx_send,
     rs_send, rs_recv, dg_send, dg_recv, g_send, g_recv,
     ss_send, ss_recv, z_send, z_recv, xf_send, xf_recv,
-    w1_send, w1_recv, w23_send, w23_recv, w4_send, w4_recv, w5_send, w5_recv, w6_send, w6_recv,
+    w1_send, w1_recv, w2_send, w2_recv, w4_send, w4_recv, w5_send, w5_recv, w6_send, w6_recv,
 ):
     b = lax.axis_index("blk")
     rep = lax.axis_index("rep")
@@ -78,15 +78,42 @@
     idx_copy = pltpu.make_async_copy(idxv, idxs, idx_sem)
     own_load(0).start()
     own_load(1).start()
+    bar = pltpu.get_barrier_semaphore()
+    for dev in (sibling, xmate, (blkidx(0, 1, 1), rep)):
+        pl.semaphore_signal(bar, inc=1, device_id=dev, device_id_type=MESH)
+    loop(1, NZ, lambda i: pl.semaphore_signal(bar, inc=1, device_id=zdev(i), device_id_type=MESH))
+    loop(1, NREP, lambda i: pl.semaphore_signal(bar, inc=1, device_id=repdev(i), device_id_type=MESH))
+
+    own_load(0).wait()
+    own_load(1).wait()
+    pl.semaphore_wait(bar, 17)
+
+    def f_right(h, j):
+        return remote(xbuf.at[h, j], xbuf.at[h, j], xr_send.at[h, j], x_recv.at[h, j], right)
+
+    def f_left(h, j):
+        return remote(xbuf.at[h, j], xbuf.at[h, j], xl_send.at[h, j], x_recv.at[h, j], left)
+
+    def f_sib(h, j):
+        return remote(xbuf.at[h, j], xbuf.at[h, j], xs_send.at[h, j], x_recv.at[h, j], sibling)
+
+    def f_mate(h):
+        return remote(xbuf.at[h, b], xbuf.at[h, b], xx_send.at[h], x_recv.at[h, b], xmate)
+
+    def f_wait(h, j):
+        f_sib(h, j).wait_recv()
+
+    def start_own(h):
+        f_mate(h).start()
+        f_right(h, b).start()
+        f_left(h, b).start()
+        f_sib(h, b).start()
+
+    start_own(0)
+    start_own(1)
     loop(0, NBLK, lambda p: tile_load(p).start())
     w_load.start()
     ct_load.start()
-
-    bar = pltpu.get_barrier_semaphore()
-    for dev in (sibling, xmate):
-        pl.semaphore_signal(bar, inc=1, device_id=dev, device_id_type=MESH)
-    loop(1, NZ, lambda i: pl.semaphore_signal(bar, inc=1, device_id=zdev(i), device_id_type=MESH))
-    loop(1, NREP, lambda i: pl.semaphore_signal(bar, inc=1, device_id=repdev(i), device_id_type=MESH))
 
     def first_pos(j):
         cj, xj, zj = j & 1, (j >> 1) & 1, j >> 2
@@ -119,34 +146,6 @@
         sbuf[h, POS] = jnp.zeros((TILE, TILE), F32)
     degs[POS] = jnp.zeros((8, TILE), F32)
 
-    own_load(0).wait()
-    own_load(1).wait()
-    pl.semaphore_wait(bar, 16)
-
-    def f_right(h, j):
-        return remote(xbuf.at[h, j], xbuf.at[h, j], xr_send.at[h, j], x_recv.at[h, j], right)
-
-    def f_left(h, j):
-        return remote(xbuf.at[h, j], xbuf.at[h, j], xl_send.at[h, j], x_recv.at[h, j], left)
-
-    def f_sib(h, j):
-        return remote(xbuf.at[h, j], xbuf.at[h, j], xs_send.at[h, j], x_recv.at[h, j], sibling)
-
-    def f_mate(h):
-        return remote(xbuf.at[h, b], xbuf.at[h, b], xx_send.at[h], x_recv.at[h, b], xmate)
-
-    def f_wait(h, j):
-        f_sib(h, j).wait_recv()
-
-    def start_own(h):
-        f_mate(h).start()
-        f_right(h, b).start()
-        f_left(h, b).start()
-        f_sib(h, b).start()
-
-    start_own(0)
-    start_own(1)
-    idx_copy.wait()
 
     def prep(p, j):
         tile_load(p).wait()
@@ -213,13 +212,14 @@
     def forward_close(h):
         def far(xq):
             j = blkidx(4, xq, 0)
+            loop(20 + xq * 4, 24 + xq * 4, lambda p: process(h, p))
             f_wait(h, j)
             f_sib(h, j).start()
-            loop(20 + xq * 4, 24 + xq * 4, lambda p: process(h, p))
 
         loop(0, 2, far)
         loop(28, 32, lambda p: process(h, p))
 
+    def send_sums(h):
         def chunk(i):
             r = rem(rep + i, NREP)
             for t in range(2):
@@ -238,13 +238,16 @@
 
     forward_open(0)
     forward_open(1)
+    idx_copy.wait()
     for k in range(1, 4):
         forward_step(0, k)
         if k > 1:
             forward_step(1, k - 1)
     forward_close(0)
+    send_sums(0)
     forward_step(1, 3)
     forward_close(1)
+    send_sums(1)
 
     w_load.wait()
     ct_load.wait()
@@ -293,8 +296,15 @@
     def w1_arrival(r):
         return remote(wp_src.at[r], wp_dst.at[r], w1_send.at[r], w1_recv.at[r], (b, r))
 
-    w2_copy = remote(w2s, w2r, w23_send.at[0], w23_recv.at[0], sibling)
-    w3_copy = remote(w3s, w3r, w23_send.at[1], w23_recv.at[1], xmate)
+    quad = xh * 2 + c
+    others = ((0, 1), (1, 0), (1, 1))
+
+    def w2_copy(xq, cq):
+        return remote(w2g.at[quad], w2g.at[quad], w2_send.at[xq * 2 + cq], w2_recv.at[quad], (blkidx(0, xq, cq), rep))
+
+    def w2_arrival(xq, cq):
+        i = rem(xh + xq, 2) * 2 + rem(c + cq, 2)
+        return remote(w2g.at[i], w2g.at[i], w2_send.at[0], w2_recv.at[i], sibling)
 
     def w4_copy(i):
         zz = rem(z + i, NZ)
@@ -317,23 +327,19 @@
 
     part = lax.dot_general(mixed[...], act_grad, (((0,), (0,)), ((), ())), preferred_element_type=F32)
     for r in range(NREP):
-        wp_src[r] = part[r * 32:(r + 1) * 32]
-    loop(1, NREP, lambda i: w1_copy(rem(rep + i, NREP)).start())
+        wp_src[r] = part[r * 32:(r + 1) * 32].astype(BF16)
 
     def w_step2():
         loop(1, NREP, lambda i: w1_arrival(rem(rep + i, NREP)).wait_recv())
         wp_dst[rep] = wp_src[rep]
-        w2s[...] = sum(wp_dst[r] for r in range(NREP))
-        w2_copy.start()
-
-    def w_step3():
-        w2_copy.wait_recv()
-        w3s[...] = w2s[...] + w2r[...]
-        w3_copy.start()
+        w2g[quad] = sum(wp_dst[r].astype(F32) for r in range(NREP))
+        for xq, cq in others:
+            w2_copy(xq, cq).start()
 
     def w_step4():
-        w3_copy.wait_recv()
-        both = w3s[...] + w3r[...]
+        for xq, cq in others:
+            w2_arrival(xq, cq).wait_recv()
+        both = (w2g[0] + w2g[1]) + (w2g[2] + w2g[3])
         for k in range(NZ):
             w4s[k] = both[(k // 2) * 8:(k // 2) * 8 + 8, (k % 2) * TILE:(k % 2) * TILE + TILE]
         loop(1, NZ, lambda i: w4_copy(i).start())
@@ -376,8 +382,8 @@
     def z_value(h, d, m, xq):
         return zr[h, (d * 4 + m) * 2 + xq].astype(F32)
 
-    def x_copy(h):
-        return remote(xs.at[h], xr.at[h], xf_send.at[h], xf_recv.at[h], xmate)
+    def x_copy(h, k):
+        return remote(xs.at[h, k], xr.at[h, k], xf_send.at[h, k], xf_recv.at[h, k], xmate)
 
     def sib_term(h, d, m, xq):
         dz = m * (1 - 2 * d)
@@ -385,127 +391,141 @@
         ss[h, k] = out_t(h, blkidx(dz, xq, 1)).astype(BF16)
         sib_copy(h, k).start()
 
-    def own_term(h, d, m, xq, first):
+    def own_term(h, d, m, xq):
         dz = m * (1 - 2 * d)
-        k = rem(dz + 8, 8) * 2 + xq
+        zrel = rem(dz + 8, 8)
+        k = zrel * 2 + xq
         value = out_t(h, blkidx(dz, xq, 0))
         sib_copy(h, k).wait_recv()
         value = value + sr[h, k].astype(F32)
-        if not first:
-            return value, k
-        zs[h, (d * 4 + m - 1) * 2 + xq] = value.astype(BF16)
+        if h == 1 and xq == 0:
+            x_copy(h, zrel).wait_recv()
+            value = value + xr[h, zrel].astype(F32)
+        return value
+
+    def cross_term(d, m):
+        zrel = rem(m * (1 - 2 * d) + 8, 8)
+        xs[1, zrel] = own_term(1, d, m, 1).astype(BF16)
+        x_copy(1, zrel).start()
+
+    def start_on(h, d, m, xq):
+        zs[h, (d * 4 + m - 1) * 2 + xq] = own_term(h, d, m, xq).astype(BF16)
         z_copy(h, d, m, xq).start()
 
     def pass_on(h, d, m, xq):
-        value, _ = own_term(h, d, m, xq, False)
+        value = own_term(h, d, m, xq)
         i = (d * 4 + m) * 2 + xq
         z_arrival(h, d, m, xq).wait_recv()
         zs[h, i - 2] = (value + zr[h, i].astype(F32)).astype(BF16)
         z_copy(h, d, m, xq).start()
 
-    def backward_open(h):
-        long, short = h, 1 - h
+    def arrive(h):
         loop(1, NREP, lambda i: g_arrival(h, rem(rep + i, NREP)).wait_recv())
-        loop(0, 2, lambda q: sib_term(h, long, 4, q))
-        loop(0, 2, lambda q: sib_term(h, short, 3, q))
-        loop(0, 2, lambda q: own_term(h, long, 4, q, True))
-        loop(0, 2, lambda q: sib_term(h, long, 3, q))
-        loop(0, 2, lambda q: own_term(h, short, 3, q, True))
-
-    def backward_third(h):
-        def third(q):
-            sib_term(h, 0, 2, q)
-            sib_term(h, 1, 2, q)
-            pass_on(h, h, 3, q)
-
-        loop(0, 2, third)
-
-    def backward_second(h):
-        def second(e):
+
+    def open_0():
+        arrive(0)
+        loop(1, NREP, lambda i: w1_copy(rem(rep + i, NREP)).start())
+        loop(0, 2, lambda q: sib_term(0, 0, 4, q))
+        loop(0, 2, lambda q: sib_term(0, 1, 3, q))
+        loop(0, 2, lambda q: start_on(0, 0, 4, q))
+        loop(0, 2, lambda q: sib_term(0, 0, 3, q))
+        loop(0, 2, lambda q: start_on(0, 1, 3, q))
+
+    def open_1():
+        arrive(1)
+        loop(0, 2, lambda q: sib_term(1, 1, 4, 1 - q))
+        loop(0, 4, lambda e: sib_term(1, rem(e, 2), 3, 1 - div(e, 2)))
+        cross_term(1, 4)
+        loop(0, 2, lambda d: cross_term(d, 3))
+        loop(0, 4, lambda e: sib_term(1, rem(e, 2), 2, 1 - div(e, 2)))
+
+    def third_0():
+        def body(q):
+            sib_term(0, 0, 2, q)
+            sib_term(0, 1, 2, q)
+            pass_on(0, 0, 3, q)
+
+        loop(0, 2, body)
+
+    def second_0():
+        def body(e):
             d, q = rem(e, 2), div(e, 2)
-            sib_term(h, d, 1, q)
-            pass_on(h, d, 2, q)
-
-        loop(0, 4, second)
-
-    def backward_first(h):
-        loop(0, 2, lambda q: sib_term(h, 0, 0, q))
-        loop(0, 4, lambda e: pass_on(h, rem(e, 2), 1, div(e, 2)))
+            sib_term(0, d, 1, q)
+            pass_on(0, d, 2, q)
+
+        loop(0, 4, body)
+
+    def first_0():
+        loop(0, 2, lambda q: sib_term(0, 0, 0, q))
+        loop(0, 4, lambda e: pass_on(0, rem(e, 2), 1, div(e, 2)))
+
+    def third_1():
+        loop(0, 2, lambda d: cross_term(d, 2))
+        loop(0, 4, lambda e: sib_term(1, rem(e, 2), 1, 1 - div(e, 2)))
+        start_on(1, 1, 4, 0)
+        start_on(1, 0, 3, 0)
+
+    def second_1():
+        loop(0, 2, lambda d: cross_term(d, 1))
+        loop(0, 2, lambda q: sib_term(1, 0, 0, 1 - q))
+        pass_on(1, 1, 3, 0)
+
+    def first_1():
+        cross_term(0, 0)
+        loop(0, 2, lambda d: pass_on(1, d, 2, 0))
+
+    def last_1():
+        loop(0, 2, lambda d: pass_on(1, d, 1, 0))
 
     def settled(h, xq):
-        value, _ = own_term(h, 0, 0, xq, False)
+        value = own_term(h, 0, 0, xq)
         z_arrival(h, 0, 0, xq).wait_recv()
         z_arrival(h, 1, 0, xq).wait_recv()
         return value + z_value(h, 0, 0, xq) + z_value(h, 1, 0, xq)
 
-    def to_mate(h):
-        xs[h] = settled(h, 1).astype(BF16)
-        x_copy(h).start()
+    def to_mate():
+        xs[0, 0] = settled(0, 1).astype(BF16)
+        x_copy(0, 0).start()
 
     def finish(h):
-        value = settled(h, 0)
-        x_copy(h).wait_recv()
-        value = value + xr[h].astype(F32) + ngt[h].astype(F32)
+        value = settled(h, 0) + ngt[h].astype(F32)
+        if h == 0:
+            x_copy(0, 0).wait_recv()
+            value = value + xr[0, 0].astype(F32)
         fgrad_ref[:, h * TILE:(h + 1) * TILE] = jnp.transpose(value).astype(BF16)
 
-    backward_open(0)
-    w_step2()
-    backward_open(1)
-    w_step3()
-    backward_third(0)
-    backward_third(1)
-    w_step4()
-    backward_second(0)
-    backward_second(1)
-    w_step5()
-    backward_first(0)
-    backward_first(1)
-    w_step6()
-    to_mate(0)
-    to_mate(1)
-    w_step7()
-    finish(0)
-    finish(1)
-
-    for h in range(2):
-        far_r, far_l = 4 - h, 3 + h
+    def drain_forward(h):
         f_mate(h).wait_send()
 
-        def drain_f(e):
+        def near(e):
             k, xq = div(e, 2), rem(e, 2)
             f_right(h, blkidx(-k, xq, 0)).wait_send()
             f_left(h, blkidx(k, xq, 0)).wait_send()
 
-        loop(0, 6, drain_f)
-
-        def drain_long(xq):
+        def farthest(xq):
             if h == 0:
                 f_right(h, blkidx(-3, xq, 0)).wait_send()
             else:
                 f_left(h, blkidx(3, xq, 0)).wait_send()
-            z_copy(h, h, 4, xq).wait_send()
-
-        loop(0, 2, drain_long)
-
-        def drain_s(e):
-            f_sib(h, blkidx(div(e, 2), rem(e, 2), 0)).wait_send()
-            sib_copy(h, e).wait_send()
-
-        loop(0, 16, drain_s)
-
-        def drain_z(e):
-            z_copy(h, rem(e, 2), 1 + div(e, 4), rem(div(e, 2), 2)).wait_send()
-
-        loop(0, 12, drain_z)
-        x_copy(h).wait_send()
-
-        def drain_rep(i):
-            rs_copy(h, rem(rep + i, NREP)).wait_send()
-            g_copy(h, i).wait_send()
-
-        loop(1, NREP, drain_rep)
-
-    def drain_w(i):
+
+        loop(0, 6, near)
+        loop(0, 2, farthest)
+        loop(0, 16, lambda e: f_sib(h, blkidx(div(e, 2), rem(e, 2), 0)).wait_send())
+        loop(1, NREP, lambda i: rs_copy(h, rem(rep + i, NREP)).wait_send())
+
+    def drain_backward(h):
+        cols = 2 - h
+
+        def near(e):
+            z_copy(h, rem(e, 2), 1 + div(e, 2 * cols), rem(div(e, 2), cols)).wait_send()
+
+        loop(0, 6 * cols, near)
+        loop(0, cols, lambda xq: z_copy(h, h, 4, xq).wait_send())
+        loop(0, NZ if h else 1, lambda k: x_copy(h, k).wait_send())
+        loop(0, 16, lambda e: sib_copy(h, e).wait_send())
+        loop(1, NREP, lambda i: g_copy(h, i).wait_send())
+
+    def drain_weight(i):
         r = rem(rep + i, NREP)
         dg_copy(r).wait_send()
         w1_copy(r).wait_send()
@@ -513,9 +533,30 @@
         w5_copy(i).wait_send()
         w6_copy(i).wait_send()
 
-    loop(1, NREP, drain_w)
-    w2_copy.wait_send()
-    w3_copy.wait_send()
+    drain_forward(0)
+    drain_forward(1)
+    open_0()
+    open_1()
+    third_0()
+    w_step2()
+    third_1()
+    second_0()
+    w_step4()
+    second_1()
+    first_0()
+    w_step5()
+    first_1()
+    to_mate()
+    w_step6()
+    last_1()
+    drain_backward(0)
+    drain_backward(1)
+    finish(0)
+    w_step7()
+    finish(1)
+    loop(1, NREP, drain_weight)
+    for xq, cq in others:
+        w2_copy(xq, cq).wait_send()
 
 
 def place_kernel(a, b, c, out_a, out_b, out_c):
@@ -564,14 +605,11 @@
             vmem((2, 16, half, width), BF16),
             vmem((2, 16, half, width), BF16),
             vmem((2, 16, half, width), BF16),
-            vmem((2, half, width), BF16),
-            vmem((2, half, width), BF16),
-            vmem((NREP, 32, width), F32),
-            vmem((NREP, 32, width), F32),
-            vmem((32, width), F32),
-            vmem((32, width), F32),
-            vmem((32, width), F32),
-            vmem((32, width), F32),
+            vmem((2, NZ, half, width), BF16),
+            vmem((2, NZ, half, width), BF16),
+            vmem((NREP, 32, width), BF16),
+            vmem((NREP, 32, width), BF16),
+            vmem((4, 32, width), F32),
             vmem((NZ, 8, TILE), F32),
             vmem((NZ, 8, TILE), F32),
             vmem((8, TILE), F32),
@@ -581,8 +619,8 @@
             dma((4,)), dma((NBLK,)), dma,
             dma((2, NBLK)), dma((2, NBLK)), dma((2, NBLK)), dma((2, NBLK)), dma((2,)),
             dma((2, NREP)), dma((2, NREP)), dma((NREP,)), dma((NREP,)), dma((2, NREP)), dma((2, NREP)),
-            dma((2, 16)), dma((2, 16)), dma((2, 16)), dma((2, 16)), dma((2,)), dma((2,)),
-            dma((NREP,)), dma((NREP,)), dma((2,)), dma((2,)), dma((NZ,)), dma((NZ,)), dma((NZ,)), dma((NZ,)),
+            dma((2, 16)), dma((2, 16)), dma((2, 16)), dma((2, 16)), dma((2, NZ)), dma((2, NZ)),
+            dma((NREP,)), dma((NREP,)), dma((4,)), dma((4,)), dma((NZ,)), dma((NZ,)), dma((NZ,)), dma((NZ,)),
             dma((NREP,)), dma((NREP,)),
         ],
         compiler_params=pltpu.CompilerParams(

time: 106 us -> 100 us (0.943); the launches traced: 104 us -> 99.8 us
  Pallas kernels: 104 us -> 99.1 us
    pallas_call x1, Pallas kernels: 102 us -> 97.3 us  [shards(): pl.pallas_call(layer_kernel, out_shape=[jax.ShapeDtypeStruct((width, widt...]
where the time goes in v4:
time: 100 us; the launch traced here: 99.8 us
  Pallas kernels  99.1 us (99%)
    pallas_call x1, Pallas kernels, shards(): pl.pallas_call(layer_kernel, out_shape=[jax.ShapeDtypeStruct((width, widt...  97.3 us

profile of v4, /device:TPU:8, one launch (start us, length us, event | category | flops | bytes accessed | tf_op | source)
XLA Modules:
  0.0 99.8 jit_solution(16409313996396957641)
XLA Ops:
  0.6 97.3 %graph_layer.1 = (bf16[256,256]{1,0:T(8,128)(2,1)}, bf16[256,256]{1,0:T(8,128)(2,1)}, f32[256,256]{1,0:T(8,128)}) custom-call(s32[4,32]{1,0:T(4,128)} %bitcast.9, s32[4,32]{1,0:T(4,128)} %bitcast.11, s32[32]{0:T(128)} %bitcast.12, s32[4,32]{1,0:T(4,128)} %bitcast.10, bf16[256,256]{1,0:T(8,128)(2,1)} %x_hbm.1, bf16[256,256]{1,0:T(8,128)(2,1)} %w_hbm.1, ...), custom_call_target="tpu_custom_call" | custom-call | flops 4294967296 | bytes 9437184 | tf_op jit(solution)/shard_map/graph_layer/pallas_call | solution.py:576
  97.9 1.9 %place.1 = (bf16[256,256]{1,0:T(8,128)(2,1)}, bf16[256,256]{1,0:T(8,128)(2,1)}, f32[256,256]{1,0:T(8,128)}) custom-call(bf16[256,256]{1,0:T(8,128)(2,1)} %get-tuple-element.6.a, bf16[256,256]{1,0:T(8,128)(2,1)} %get-tuple-element.7.b, f32[256,256]{1,0:T(8,128)} %get-tuple-element.8.c), custom_call_target="tpu_custom_call" | custom-call | tf_op jit(solution)/shard_map/place/pallas_call | solution.py:634

commit v5 on v4

--- a/solution.py
+++ b/solution.py
@@ -104,11 +104,12 @@
         f_sib(h, j).wait_recv()
 
     def start_own(h):
-        f_mate(h).start()
         f_right(h, b).start()
         f_left(h, b).start()
         f_sib(h, b).start()
 
+    f_mate(0).start()
+    f_mate(1).start()
     start_own(0)
     start_own(1)
     loop(0, NBLK, lambda p: tile_load(p).start())
@@ -212,9 +213,9 @@
     def forward_close(h):
         def far(xq):
             j = blkidx(4, xq, 0)
-            loop(20 + xq * 4, 24 + xq * 4, lambda p: process(h, p))
             f_wait(h, j)
             f_sib(h, j).start()
+            loop(20 + xq * 4, 24 + xq * 4, lambda p: process(h, p))
 
         loop(0, 2, far)
         loop(28, 32, lambda p: process(h, p))
@@ -270,7 +271,6 @@
             mixed[pl.ds(t * TILE, TILE), h * TILE:(h + 1) * TILE] = (part * scale_col[t]).astype(BF16)
     pre = jnp.dot(mixed[...], wbuf[...], preferred_element_type=F32)
     sig = 1.0 / (1.0 + jnp.exp(-pre))
-    act_ref[...] = (pre * sig).astype(BF16)
     act_grad = (ctbuf[...].astype(F32) * sig * (1.0 + pre * (1.0 - sig))).astype(BF16)
 
     def g_copy(h, i):
@@ -325,6 +325,7 @@
     def w6_arrival(r):
         return remote(w6s, w6r.at[r], w6_send.at[0], w6_recv.at[r], (b, r))
 
+    act_ref[...] = (pre * sig).astype(BF16)
     part = lax.dot_general(mixed[...], act_grad, (((0,), (0,)), ((), ())), preferred_element_type=F32)
     for r in range(NREP):
         wp_src[r] = part[r * 32:(r + 1) * 32].astype(BF16)

time: 100 us -> 99.7 us (level)
  no operation moved by 1% of the time
where the time goes in v5:
time: 99.7 us; the launch traced here: 99.5 us
  Pallas kernels  98.9 us (99%)
    pallas_call x1, Pallas kernels, shards(): pl.pallas_call(layer_kernel, out_shape=[jax.ShapeDtypeStruct((width, widt...  97 us

profile of v5, /device:TPU:8, one launch (start us, length us, event | category | flops | bytes accessed | tf_op | source)
XLA Modules:
  0.0 99.5 jit_solution(11256264354046152136)
XLA Ops:
  0.6 97.0 %graph_layer.1 = (bf16[256,256]{1,0:T(8,128)(2,1)}, bf16[256,256]{1,0:T(8,128)(2,1)}, f32[256,256]{1,0:T(8,128)}) custom-call(s32[4,32]{1,0:T(4,128)} %bitcast.9, s32[4,32]{1,0:T(4,128)} %bitcast.11, s32[32]{0:T(128)} %bitcast.12, s32[4,32]{1,0:T(4,128)} %bitcast.10, bf16[256,256]{1,0:T(8,128)(2,1)} %x_hbm.1, bf16[256,256]{1,0:T(8,128)(2,1)} %w_hbm.1, ...), custom_call_target="tpu_custom_call" | custom-call | flops 4294967296 | bytes 9437184 | tf_op jit(solution)/shard_map/graph_layer/pallas_call | solution.py:577
  97.6 1.9 %place.1 = (bf16[256,256]{1,0:T(8,128)(2,1)}, bf16[256,256]{1,0:T(8,128)(2,1)}, f32[256,256]{1,0:T(8,128)}) custom-call(bf16[256,256]{1,0:T(8,128)(2,1)} %get-tuple-element.6.a, bf16[256,256]{1,0:T(8,128)(2,1)} %get-tuple-element.7.b, f32[256,256]{1,0:T(8,128)} %get-tuple-element.8.c), custom_call_target="tpu_custom_call" | custom-call | tf_op jit(solution)/shard_map/place/pallas_call | solution.py:635

commit v6 on v5

--- a/solution.py
+++ b/solution.py
@@ -442,17 +442,17 @@
 
     def third_0():
         def body(q):
+            pass_on(0, 0, 3, q)
             sib_term(0, 0, 2, q)
             sib_term(0, 1, 2, q)
-            pass_on(0, 0, 3, q)
 
         loop(0, 2, body)
 
     def second_0():
         def body(e):
             d, q = rem(e, 2), div(e, 2)
+            pass_on(0, d, 2, q)
             sib_term(0, d, 1, q)
-            pass_on(0, d, 2, q)
 
         loop(0, 4, body)
 
@@ -472,8 +472,8 @@
         pass_on(1, 1, 3, 0)
 
     def first_1():
+        loop(0, 2, lambda d: pass_on(1, d, 2, 0))
         cross_term(0, 0)
-        loop(0, 2, lambda d: pass_on(1, d, 2, 0))
 
     def last_1():
         loop(0, 2, lambda d: pass_on(1, d, 1, 0))

time: 99.7 us -> 99.3 us (level)
  no operation moved by 1% of the time
where the time goes in v6:
time: 99.3 us; the launch traced here: 99.1 us
  Pallas kernels  98.5 us (99%)
    pallas_call x1, Pallas kernels, shards(): pl.pallas_call(layer_kernel, out_shape=[jax.ShapeDtypeStruct((width, widt...  96.6 us

profile of v6, /device:TPU:8, one launch (start us, length us, event | category | flops | bytes accessed | tf_op | source)
XLA Modules:
  0.0 99.1 jit_solution(8697852904786630382)
XLA Ops:
  0.6 96.6 %graph_layer.1 = (bf16[256,256]{1,0:T(8,128)(2,1)}, bf16[256,256]{1,0:T(8,128)(2,1)}, f32[256,256]{1,0:T(8,128)}) custom-call(s32[4,32]{1,0:T(4,128)} %bitcast.9, s32[4,32]{1,0:T(4,128)} %bitcast.11, s32[32]{0:T(128)} %bitcast.12, s32[4,32]{1,0:T(4,128)} %bitcast.10, bf16[256,256]{1,0:T(8,128)(2,1)} %x_hbm.1, bf16[256,256]{1,0:T(8,128)(2,1)} %w_hbm.1, ...), custom_call_target="tpu_custom_call" | custom-call | flops 4294967296 | bytes 9437184 | tf_op jit(solution)/shard_map/graph_layer/pallas_call | solution.py:577
  97.2 1.9 %place.1 = (bf16[256,256]{1,0:T(8,128)(2,1)}, bf16[256,256]{1,0:T(8,128)(2,1)}, f32[256,256]{1,0:T(8,128)}) custom-call(bf16[256,256]{1,0:T(8,128)(2,1)} %get-tuple-element.6.a, bf16[256,256]{1,0:T(8,128)(2,1)} %get-tuple-element.7.b, f32[256,256]{1,0:T(8,128)} %get-tuple-element.8.c), custom_call_target="tpu_custom_call" | custom-call | tf_op jit(solution)/shard_map/place/pallas_call | solution.py:635
